TPU v7x, 256 devices: a whole 4x4x8 slice. The times are simulated.
256 devices in a mesh: dp: 32 (over z, y), ctx: 8 (over x, core).
Axes of the slice: x: 4, y: 4, z: 8, core: 2. Of those that a mesh axis runs over, the one named last changes fastest.
Arguments:
- queries: bfloat16 [32, 1024, 8192], P('dp', 'ctx'), may hold values from -100 to 100
- keys: bfloat16 [32, 1024, 1024], P('dp', 'ctx'), may hold values from -8 to 8
- values: bfloat16 [32, 1024, 1024], P('dp', 'ctx'), may hold values from -6 to 6
- upstream: bfloat16 [32, 1024, 8192], P('dp', 'ctx'), may hold values from -0.6 to 0.6
- token_logp: float32 [32, 1024], P('dp', 'ctx'), may hold values from -4 to -0.05
- segments: int32 [32, 1024], replicated, may hold values from 0 to 3, as said below
- partner: int32 [128], replicated, may hold values from 0 to 127, as said below
- chosen: int32 [128], replicated, may hold values from 0 to 1, as said below
- ref_score: float32 [128], replicated, may hold values from -1 to 1
Outputs:
- grad_q: bfloat16 [32, 1024, 8192], P('dp', 'ctx')
- grad_k: bfloat16 [32, 1024, 1024], P('dp', 'ctx')
- grad_v: bfloat16 [32, 1024, 1024], P('dp', 'ctx')
- loss: float32 [], replicated
Inputs may be any that keep to these rules, and one draw needn't show every extreme that they name: `segments`: segment numbers never fall along a pack and each of the 4 numbers appears in every pack; in every pack one sequence has exactly 512 tokens and every other one at least (512) // 6. partner[partner[g]] = g and partner[g] != g; every sequence lies in exactly one pair. `chosen`: exactly one sequence of each pair has 1.
All inputs are finite; a program needn't handle non-finite values.
Results may differ from a plain program's by a relative error of at most 0.022.
Values may be sent and summed in bfloat16 or wider, within the bound.
No kernel may reach another device: no remote copies, remote signals or barrier semaphores. Data moves between devices by JAX's collectives and lax.ppermute only.
A program may use at most 128 MiB of HBM per device.

v0:
```python
import math

import jax
import jax.numpy as jnp
from jax import lax
from jax.sharding import PartitionSpec as P

HD = 128
SEQS = 4


NEG_FILL = -1e30
BETA = 2.0
LOSS_SCALE = 1024.0


def block_rows(rows, heads):
    return math.gcd(rows, min(512, max(8, 4096 // heads)))


def allowed_block(q_pos, q_seg, k_seg, first, top, upto):
    cols = jnp.arange(upto, dtype=jnp.int32)
    allowed = cols[None, :] <= q_pos[first:top][:, None]
    return allowed & (k_seg[:upto][None, :] == q_seg[first:top][:, None])


def attend_forward(q_rows, k_all, v_all, q_pos, q_seg, k_seg):
    rows = q_rows.shape[0]
    keys_total = k_all.shape[0]
    kv_count = k_all.shape[1] // HD
    group = q_rows.shape[1] // k_all.shape[1]
    block = block_rows(rows, kv_count * group)
    scale = HD ** (-0.5)
    q_four = q_rows.reshape(rows, kv_count, group, HD)
    k_three = k_all.reshape(keys_total, kv_count, HD)
    v_three = v_all.reshape(keys_total, kv_count, HD)
    probs = []
    outputs = []
    for index in range(rows // block):
        first = index * block
        top = first + block
        scores = (
            jnp.einsum(
                "qkgd,skd->kgqs",
                q_four[first:top],
                k_three[:top],
                preferred_element_type=jnp.float32,
            )
            * scale
        )
        allowed = allowed_block(q_pos, q_seg, k_seg, first, top, top)
        scores = jnp.where(allowed[None, None], scores, NEG_FILL)
        peak = jnp.max(scores, axis=-1, keepdims=True)
        expo = jnp.exp(scores - peak)
        weights = (expo / jnp.sum(expo, axis=-1, keepdims=True)).astype(jnp.bfloat16)
        outputs.append(
            jnp.einsum("kgqs,skd->qkgd", weights, v_three[:top], preferred_element_type=jnp.float32)
        )
        probs.append(weights)
    return (probs, jnp.concatenate(outputs, axis=0))


def attend_backward(q_rows, k_all, v_all, probs, outputs, grad_out):
    rows = q_rows.shape[0]
    keys_total = k_all.shape[0]
    kv_count = k_all.shape[1] // HD
    group = q_rows.shape[1] // k_all.shape[1]
    block = block_rows(rows, kv_count * group)
    scale = HD ** (-0.5)
    q_four = q_rows.reshape(rows, kv_count, group, HD)
    k_three = k_all.reshape(keys_total, kv_count, HD)
    v_three = v_all.reshape(keys_total, kv_count, HD)
    key_grad = jnp.zeros((keys_total, kv_count, HD), jnp.float32)
    value_grad = jnp.zeros((keys_total, kv_count, HD), jnp.float32)
    query_parts = []
    for index in range(rows // block):
        first = index * block
        top = first + block
        weights = probs[index]
        dout = grad_out[first:top]
        rest = ((0, keys_total - top), (0, 0), (0, 0))
        value_grad = value_grad + jnp.pad(
            jnp.einsum("kgqs,qkgd->skd", weights, dout, preferred_element_type=jnp.float32), rest
        )
        dprob = jnp.einsum(
            "qkgd,skd->kgqs", dout, v_three[:top], preferred_element_type=jnp.float32
        )
        delta = jnp.sum(dout.astype(jnp.float32) * outputs[first:top], axis=-1)
        delta = jnp.transpose(delta, (1, 2, 0))[..., None]
        dscore = (weights.astype(jnp.float32) * (dprob - delta) * scale).astype(jnp.bfloat16)
        query_parts.append(
            jnp.einsum("kgqs,skd->qkgd", dscore, k_three[:top], preferred_element_type=jnp.float32)
        )
        key_grad = key_grad + jnp.pad(
            jnp.einsum(
                "kgqs,qkgd->skd", dscore, q_four[first:top], preferred_element_type=jnp.float32
            ),
            rest,
        )
    query_grad = jnp.concatenate(query_parts, axis=0).reshape(rows, -1)
    return (
        query_grad.astype(jnp.bfloat16),
        key_grad.reshape(keys_total, -1),
        value_grad.reshape(keys_total, -1),
    )


def per_device(queries, keys, values, upstream, token_logp, segments, partner, chosen, ref_score):
    ctx_size = lax.axis_size("ctx")
    dp_size = lax.axis_size("dp")
    rank = lax.axis_index("dp")
    place = lax.axis_index("ctx")
    tok_count = queries.shape[1]
    pack = tok_count * ctx_size
    total = dp_size * SEQS
    slots = jnp.arange(SEQS, dtype=jnp.int32)
    ids = jnp.arange(total, dtype=jnp.int32)
    counts = jnp.sum((segments[:, :, None] == slots[None, None, :]).astype(jnp.int32), axis=1)
    lengths = counts.reshape(total).astype(jnp.float32)
    own_seg = lax.dynamic_index_in_dim(segments, rank, 0, keepdims=False)
    tok_seg = lax.dynamic_slice_in_dim(own_seg, place * tok_count, tok_count)
    q_rows, k_all, v_all, u_rows = (
        lax.all_to_all(queries[0], "ctx", split_axis=1, concat_axis=0, tiled=True),
        lax.all_to_all(keys[0], "ctx", split_axis=1, concat_axis=0, tiled=True),
        lax.all_to_all(values[0], "ctx", split_axis=1, concat_axis=0, tiled=True),
        lax.all_to_all(upstream[0], "ctx", split_axis=1, concat_axis=0, tiled=True),
    )
    q_pos = jnp.arange(pack, dtype=jnp.int32)
    rows = q_rows.shape[0]
    kv_count = k_all.shape[1] // HD
    group = q_rows.shape[1] // k_all.shape[1]
    u_four = u_rows.reshape(rows, kv_count, group, HD)
    probs, outputs = attend_forward(q_rows, k_all, v_all, q_pos, own_seg, own_seg)
    hit_rows = (own_seg[:, None] == slots[None, :]).astype(jnp.float32)
    row_term = jnp.sum(outputs * u_four, axis=(1, 2, 3))
    attend_part = jnp.sum(row_term[:, None] * hit_rows, axis=0)
    logp_part = jnp.sum(
        token_logp[0][:, None] * (tok_seg[:, None] == slots[None, :]).astype(jnp.float32), axis=0
    )
    contribution = jnp.where(ids // SEQS == rank, jnp.tile(attend_part + logp_part, dp_size), 0.0)
    totals = lax.psum(contribution, ("dp", "ctx"))
    adjusted = totals / lengths - ref_score
    match = (partner[:, None] == ids[None, :]).astype(jnp.float32)
    mate_adjusted = jnp.sum(match * adjusted[None, :], axis=1)
    sign = 2.0 * chosen.astype(jnp.float32) - 1.0
    margin = BETA * sign * (adjusted - mate_adjusted)
    loss = jnp.sum(chosen.astype(jnp.float32) * jax.nn.softplus(-margin))
    weight = -sign * BETA * jax.nn.sigmoid(-margin) * LOSS_SCALE / lengths
    own_weight = lax.dynamic_slice_in_dim(weight, rank * SEQS, SEQS)
    token_weight = jnp.sum(hit_rows * own_weight[None, :], axis=1)
    grad_out = (token_weight[:, None, None, None] * u_four).astype(jnp.bfloat16)
    grad_q, key_terms, value_terms = attend_backward(q_rows, k_all, v_all, probs, outputs, grad_out)
    tok_q, tok_k, tok_v = (
        lax.all_to_all(grad_q, "ctx", split_axis=0, concat_axis=1, tiled=True),
        lax.all_to_all(
            key_terms.astype(jnp.bfloat16), "ctx", split_axis=0, concat_axis=1, tiled=True
        ),
        lax.all_to_all(
            value_terms.astype(jnp.bfloat16), "ctx", split_axis=0, concat_axis=1, tiled=True
        ),
    )
    return (tok_q[None], tok_k[None], tok_v[None], loss)


def solution(mesh):
    return jax.shard_map(
        per_device,
        mesh=mesh,
        in_specs=(
            P("dp", "ctx", None),
            P("dp", "ctx", None),
            P("dp", "ctx", None),
            P("dp", "ctx", None),
            P("dp", "ctx"),
            P(),
            P(),
            P(),
            P(),
        ),
        out_specs=(P("dp", "ctx", None), P("dp", "ctx", None), P("dp", "ctx", None), P()),
        check_vma=False,
    )
```

profile of v0, /device:TPU:1, one launch (start us, length us, event | category | flops | bytes accessed | tf_op | source)
XLA Modules:
  0.0 281.5 jit_solution(13926105201098897090)
XLA Ops:
  2.5 6.6 %all-to-all-start = ((bf16[128,8,128]{2,0,1:T(8,128)(2,1)}), bf16[128,8,128]{2,0,1:T(8,128)(2,1)S(1)}, u32[]{:S(2)}, u32[]{:S(2)}) async-start(bf16[128,8,128]{2,0,1:T(8,128)(2,1)} %copy.102), calls=%async_computation | async-start | bytes 524288 | tf_op jit(solution)/shard_map/all_to_all | solution.py:124
  10.8 4.8 %all-to-all-done = bf16[128,8,128]{2,0,1:T(8,128)(2,1)S(1)} async-done(((bf16[128,8,128]{2,0,1:T(8,128)(2,1)}), bf16[128,8,128]{2,0,1:T(8,128)(2,1)S(1)}, u32[]{:S(2)}, u32[]{:S(2)}) %all-to-all-start) | async-done | bytes 262176 | tf_op jit(solution)/shard_map/all_to_all | solution.py:124
  15.6 4.4 %all-to-all-start.2 = ((bf16[128,8,128]{2,0,1:T(8,128)(2,1)}), bf16[128,8,128]{2,0,1:T(8,128)(2,1)S(1)}, u32[]{:S(2)}, u32[]{:S(2)}) async-start(bf16[128,8,128]{2,0,1:T(8,128)(2,1)} %copy.105), calls=%async_computation.2 | async-start | bytes 524288 | tf_op jit(solution)/shard_map/all_to_all | solution.py:125
  21.4 2.5 copy.103
  23.9 2.6 all-to-all-done.2
  26.5 4.5 %all-to-all-start.1 = ((bf16[128,8,1024]{2,0,1:T(8,128)(2,1)}), bf16[128,8,1024]{2,0,1:T(8,128)(2,1)S(1)}, u32[]{:S(2)}, u32[]{:S(2)}) async-start(bf16[128,8,1024]{2,0,1:T(8,128)(2,1)} %copy.103), calls=%async_computation.1 | async-start | bytes 4194304 | tf_op jit(solution)/shard_map/all_to_all | solution.py:123
  31.1 4.1 %copy.110 = bf16[1,128,8192]{1,2,0:T(8,128)(2,1)} copy(bf16[1,128,8192]{2,1,0:T(8,128)(2,1)} %param.12) | data formatting | bytes 4194304 | tf_op args[3]
  35.2 3.9 %copy.111 = bf16[128,8,1024]{2,0,1:T(8,128)(2,1)} copy(bf16[128,8,1024]{0,2,1:T(8,128)(2,1)} %bitcast.255) | data formatting | bytes 4194304 | tf_op jit(solution)/shard_map/all_to_all | solution.py:126
  42.3 15.1 %all-to-all-done.1 = bf16[128,8,1024]{2,0,1:T(8,128)(2,1)S(1)} async-done(((bf16[128,8,1024]{2,0,1:T(8,128)(2,1)}), bf16[128,8,1024]{2,0,1:T(8,128)(2,1)S(1)}, u32[]{:S(2)}, u32[]{:S(2)}) %all-to-all-start.1) | async-done | bytes 2097184 | tf_op jit(solution)/shard_map/all_to_all | solution.py:123
  58.7 4.9 %all-to-all-start.3 = ((bf16[128,8,1024]{2,0,1:T(8,128)(2,1)}), bf16[128,8,1024]{2,0,1:T(8,128)(2,1)S(1)}, u32[]{:S(2)}, u32[]{:S(2)}) async-start(bf16[128,8,1024]{2,0,1:T(8,128)(2,1)} %copy.111), calls=%async_computation.3 | async-start | bytes 4194304 | tf_op jit(solution)/shard_map/all_to_all | solution.py:126
  63.6 2.7 fusion.80
  66.6 7.3 %fusion.4 = (f32[8,512]{1,0:T(8,128)S(1)}, f32[1024,512,8]{1,0,2:T(8,128)}) fusion(pred[512,1024]{0,1:T(8,128)(4,1)S(1)} %fusion.25, bf16[1024,128,1]{1,0,2:T(8,128)(2,1)S(1)} %bitcast.264, bf16[512,8,128]{2,1,0:T(8,128)(2,1)S(1)} %bitcast.256), kind=kOutput, calls=%fused_computation.8 | convolution fusion | flops 1086320640 | bytes 18628608 | tf_op jit(solution)/shard_map/qkgd,skd->kgqs/dot_general | solution.py:43
  73.9 9.8 %fusion.3 = f32[8,512]{1,0:T(8,128)} fusion(f32[1024,512,8]{1,0,2:T(8,128)} %get-tuple-element.25, f32[8,512]{1,0:T(8,128)S(1)} %get-tuple-element.24, pred[512,1024]{0,1:T(8,128)(4,1)S(1)} %fusion.25), kind=kLoop, calls=%fused_computation.7 | loop fusion | flops 16773120 | bytes 17334272 | tf_op jit(solution)/shard_map/reduce_sum | solution.py:55
  83.7 8.1 %divide_convert_fusion = bf16[1,8,512,1024]{2,3,1,0:T(8,128)(2,1)S(1)} fusion(f32[1024,512,8]{1,0,2:T(8,128)} %get-tuple-element.25, f32[8,512]{1,0:T(8,128)} %fusion.3, f32[8,512]{1,0:T(8,128)S(1)} %get-tuple-element.24, pred[512,1024]{0,1:T(8,128)(4,1)S(1)} %fusion.25), kind=kLoop, calls=%fused_computation.5 | loop fusion | flops 20971520 | bytes 25722880 | tf_op jit(solution)/shard_map/convert_element_type | solution.py:55
  101.7 2.4 fusion.29
  105.5 4.4 %copy.109 = f32[1024,1,8,128]{3,2,0,1:T(8,128)} copy(f32[1024,1,8,128]{3,0,2,1:T(8,128)S(1)} %pad_maximum_fusion) | data formatting | bytes 8388608 | tf_op jit(solution)/shard_map/concatenate | solution.py:60
  109.9 4.9 %concatenate.12 = f32[8,128,1024]{2,1,0:T(8,128)} reshape(f32[1024,1,8,128]{3,2,0,1:T(8,128)} %copy.109) | data formatting | bytes 8388608 | tf_op jit(solution)/shard_map/concatenate | solution.py:60
  114.8 2.7 fusion.19
  117.8 80.0 %psum.7 = f32[128]{0:T(128)S(1)} all-reduce(f32[128]{0:T(128)S(1)} %compare_select_fusion.1), channel_id=1, replica_groups=mesh['dp'=32,'ctx'=8] {'dp','ctx'}, use_global_device_ids=true, to_apply=%region_7.8 | all-reduce | flops 128 | bytes 1024 | tf_op jit(solution)/shard_map/psum | solution.py:141
  205.7 2.9 %fusion.60 = bf16[16,8,8,128]{3,1,2,0:T(8,128)(2,1)S(1)} fusion(bf16[1,8,512,1024]{2,3,1,0:T(8,128)(2,1)S(1)} %bitcast.248, bf16[1024,1,8,128]{3,0,2,1:T(8,128)(2,1)S(1)} %fusion.24, f32[512,1,128]{0,2,1:T(8,128)S(1)} %fusion.57), kind=kOutput, calls=%fused_computation.55 | convolution fusion | flops 1074003968 | bytes 9961472 | tf_op jit(solution)/shard_map/kgqs,qkgd->skd/dot_general | solution.py:83
  209.5 4.5 %all-to-all-start.6 = ((bf16[8,128,128]{1,2,0:T(8,128)(2,1)}), bf16[8,128,128]{1,2,0:T(8,128)(2,1)S(1)}, u32[]{:S(2)}, u32[]{:S(2)}) async-start(bf16[8,128,128]{1,2,0:T(8,128)(2,1)} %copy.127), calls=%async_computation.6 | async-start | bytes 524288 | tf_op jit(solution)/shard_map/all_to_all | solution.py:158
  214.0 3.7 %fusion.18 = bf16[8,512,512]{1,2,0:T(8,128)(2,1)S(1)} fusion(bf16[1,8,512,512]{2,3,1,0:T(8,128)(2,1)} %copy-done.1, f32[8,512]{1,0:T(8,128)S(1)} %bitcast.280, bf16[512,128,1]{1,0,2:T(8,128)(2,1)S(1)} %bitcast.270, bf16[1024,1,8,128]{3,0,2,1:T(8,128)(2,1)S(1)} %fusion.24), kind=kOutput, calls=%fused_computation.26 | convolution fusion | flops 547356672 | bytes 9584640 | tf_op jit(solution)/shard_map/qkgd,skd->kgqs/dot_general | solution.py:85
  220.9 5.2 %fusion.2 = bf16[1,8,512,1024]{2,3,1,0:T(8,128)(2,1)S(1)} fusion(bf16[1,8,512,1024]{2,3,1,0:T(8,128)(2,1)} %copy-done, bf16[1024,128,1]{1,0,2:T(8,128)(2,1)S(1)} %bitcast.268, f32[8,512]{1,0:T(8,128)S(1)} %bitcast.285, bf16[1024,1,8,128]{3,0,2,1:T(8,128)(2,1)S(1)} %fusion.24), kind=kOutput, calls=%fused_computation.3 | convolution fusion | flops 1094713344 | bytes 18104320 | tf_op jit(solution)/shard_map/qkgd,skd->kgqs/dot_general | solution.py:85
  226.1 3.1 %fusion.54 = bf16[1024,1,128]{2,0,1:T(8,128)(2,1)} fusion(bf16[1,8,512,1024]{2,3,1,0:T(8,128)(2,1)S(1)} %fusion.2, bf16[512,8,128]{2,1,0:T(8,128)(2,1)S(1)} %bitcast.257, f32[512,1,128]{2,0,1:T(8,128)S(1)} %convolution_bitcast_fusion), kind=kOutput, calls=%fused_computation.52 | convolution fusion | flops 1074003968 | bytes 9961472 | tf_op jit(solution)/shard_map/kgqs,qkgd->skd/dot_general | solution.py:95
  229.2 2.4 fusion.35
  231.6 4.8 %all-to-all-start.5 = ((bf16[8,128,128]{2,1,0:T(8,128)(2,1)}), bf16[8,128,128]{2,1,0:T(8,128)(2,1)S(1)}, u32[]{:S(2)}, u32[]{:S(2)}) async-start(bf16[8,128,128]{2,1,0:T(8,128)(2,1)} %bitcast.71), calls=%async_computation.5 | async-start | bytes 524288 | tf_op jit(solution)/shard_map/all_to_all | solution.py:155
  236.4 3.5 %fusion.38 = bf16[512,1,8,128]{3,0,2,1:T(8,128)(2,1)S(1)} fusion(bf16[8,512,512]{1,2,0:T(8,128)(2,1)} %copy-done.7, bf16[512,128,1]{1,0,2:T(8,128)(2,1)S(1)} %bitcast.272), kind=kOutput, calls=%fused_computation.46 | convolution fusion | flops 537395200 | bytes 5373952 | tf_op jit(solution)/shard_map/kgqs,skd->qkgd/dot_general | solution.py:92
  241.4 2.3 convert_element_type.113
  243.7 4.8 %all-to-all-start.4 = ((bf16[8,128,1024]{2,1,0:T(8,128)(2,1)}), bf16[8,128,1024]{2,1,0:T(8,128)(2,1)S(1)}, u32[]{:S(2)}, u32[]{:S(2)}) async-start(bf16[8,128,1024]{2,1,0:T(8,128)(2,1)} %convert_element_type.113), calls=%async_computation.4 | async-start | bytes 4194304 | tf_op jit(solution)/shard_map/all_to_all | solution.py:154
  250.4 24.5 %all-to-all-done.4 = bf16[8,128,1024]{2,1,0:T(8,128)(2,1)S(1)} async-done(((bf16[8,128,1024]{2,1,0:T(8,128)(2,1)}), bf16[8,128,1024]{2,1,0:T(8,128)(2,1)S(1)}, u32[]{:S(2)}, u32[]{:S(2)}) %all-to-all-start.4) | async-done | bytes 2097184 | tf_op jit(solution)/shard_map/all_to_all | solution.py:154
  274.8 2.4 copy.119
  277.2 4.1 %copy.128 = bf16[1,128,8192]{2,1,0:T(8,128)(2,1)} copy(bf16[1,128,8192]{1,2,0:T(8,128)(2,1)} %bitcast.253) | data formatting | bytes 4194304
  (111 shorter events, 36.4 us)
Async XLA Ops:
  0.6 19.3 %copy-start.14 = (bf16[1,128,8192]{2,1,0:T(8,128)(2,1)S(1)}, bf16[1,128,8192]{2,1,0:T(8,128)(2,1)}, u32[]{:S(2)}) copy-start(bf16[1,128,8192]{2,1,0:T(8,128)(2,1)} %param.9) | copy-start | bytes 6291460
  2.5 13.1 %all-to-all-start = ((bf16[128,8,128]{2,0,1:T(8,128)(2,1)}), bf16[128,8,128]{2,0,1:T(8,128)(2,1)S(1)}, u32[]{:S(2)}, u32[]{:S(2)}) async-start(bf16[128,8,128]{2,0,1:T(8,128)(2,1)} %copy.102), calls=%async_computation | async-start | bytes 524288 | tf_op jit(solution)/shard_map/all_to_all | solution.py:124
  15.6 10.9 %all-to-all-start.2 = ((bf16[128,8,128]{2,0,1:T(8,128)(2,1)}), bf16[128,8,128]{2,0,1:T(8,128)(2,1)S(1)}, u32[]{:S(2)}, u32[]{:S(2)}) async-start(bf16[128,8,128]{2,0,1:T(8,128)(2,1)} %copy.105), calls=%async_computation.2 | async-start | bytes 524288 | tf_op jit(solution)/shard_map/all_to_all | solution.py:125
  26.5 30.9 %all-to-all-start.1 = ((bf16[128,8,1024]{2,0,1:T(8,128)(2,1)}), bf16[128,8,1024]{2,0,1:T(8,128)(2,1)S(1)}, u32[]{:S(2)}, u32[]{:S(2)}) async-start(bf16[128,8,1024]{2,0,1:T(8,128)(2,1)} %copy.103), calls=%async_computation.1 | async-start | bytes 4194304 | tf_op jit(solution)/shard_map/all_to_all | solution.py:123
  31.1 8.0 %copy-start.17 = (s32[32,1024]{1,0:T(8,128)S(1)}, s32[32,1024]{1,0:T(8,128)}, u32[]{:S(2)}) copy-start(s32[32,1024]{1,0:T(8,128)} %param.14) | copy-start | bytes 393220
  31.1 9.2 %copy-start.23 = (f32[1,128]{1,0:T(1,128)S(1)}, f32[1,128]{1,0:T(1,128)}, u32[]{:S(2)}) copy-start(f32[1,128]{1,0:T(1,128)} %param.13) | copy-start | bytes 1540
  40.1 2.2 copy-start.18
  58.7 56.1 %all-to-all-start.3 = ((bf16[128,8,1024]{2,0,1:T(8,128)(2,1)}), bf16[128,8,1024]{2,0,1:T(8,128)(2,1)S(1)}, u32[]{:S(2)}, u32[]{:S(2)}) async-start(bf16[128,8,1024]{2,0,1:T(8,128)(2,1)} %copy.111), calls=%async_computation.3 | async-start | bytes 4194304 | tf_op jit(solution)/shard_map/all_to_all | solution.py:126
  66.6 7.4 %copy-start.9 = (bf16[64,8,8,128]{3,2,1,0:T(8,128)(2,1)}, bf16[64,8,8,128]{3,2,1,0:T(8,128)(2,1)S(1)}, u32[]{:S(2)}) copy-start(bf16[64,8,8,128]{3,2,1,0:T(8,128)(2,1)S(1)} %copy.144) | copy-start | bytes 3145732
  83.7 8.1 %copy-start.13 = (bf16[4,128,1024]{2,1,0:T(8,128)(2,1)S(1)}, bf16[4,128,1024]{2,1,0:T(8,128)(2,1)}, u32[]{:S(2)}) copy-start(bf16[4,128,1024]{2,1,0:T(8,128)(2,1)} %get-tuple-element.18) | copy-start | bytes 3145732
  83.7 8.4 %copy-start.15 = (bf16[4,128,128]{2,1,0:T(8,128)(2,1)S(1)}, bf16[4,128,128]{2,1,0:T(8,128)(2,1)}, u32[]{:S(2)}) copy-start(bf16[4,128,128]{2,1,0:T(8,128)(2,1)} %slice.54) | copy-start | bytes 393220
  91.8 9.9 %copy-start = (bf16[1,8,512,1024]{2,3,1,0:T(8,128)(2,1)}, bf16[1,8,512,1024]{2,3,1,0:T(8,128)(2,1)S(1)}, u32[]{:S(2)}) copy-start(bf16[1,8,512,1024]{2,3,1,0:T(8,128)(2,1)S(1)} %divide_convert_fusion) | copy-start | bytes 25165828
  92.1 2.4 copy-start.11
  98.4 2.0 copy-start.1
  101.7 2.4 copy-start.3
  114.7 2.7 copy-start.19
  114.7 2.9 %copy-start.25 = (f32[4]{0:T(128)S(1)}, f32[4]{0:T(128)}, u32[]{:S(2)}) copy-start(f32[4]{0:T(128)} %select_reduce_fusion.3) | copy-start | bytes 52
  114.7 83.0 %copy-start.20 = (f32[128]{0:T(128)S(1)}, f32[128]{0:T(128)}, u32[]{:S(2)}) copy-start(f32[128]{0:T(128)} %convert_element_type.104) | copy-start | bytes 1540
  114.8 83.0 %copy-start.21 = (f32[128]{0:T(128)S(1)}, f32[128]{0:T(128)}, u32[]{:S(2)}) copy-start(f32[128]{0:T(128)} %param.17) | copy-start | bytes 1540
  114.8 83.0 %copy-start.24 = (s32[128]{0:T(128)S(1)}, s32[128]{0:T(128)}, u32[]{:S(2)}) copy-start(s32[128]{0:T(128)} %param.15) | copy-start | bytes 1540
  114.8 83.2 %copy-start.22 = (s32[128]{0:T(128)S(1)}, s32[128]{0:T(128)}, u32[]{:S(2)}) copy-start(s32[128]{0:T(128)} %param.16) | copy-start | bytes 1540
  199.2 4.7 %copy-start.6 = (f32[512,1,8,128]{3,0,2,1:T(8,128)S(1)}, f32[512,1,8,128]{3,0,2,1:T(8,128)}, u32[]{:S(2)}) copy-start(f32[512,1,8,128]{3,0,2,1:T(8,128)} %copy-done.5) | copy-start | bytes 6291460
  200.2 2.2 copy-start.2
  200.3 3.7 %copy-start.4 = (f32[512,1,8,128]{3,0,2,1:T(8,128)S(1)}, f32[512,1,8,128]{3,0,2,1:T(8,128)}, u32[]{:S(2)}) copy-start(f32[512,1,8,128]{3,0,2,1:T(8,128)} %copy-done.3) | copy-start | bytes 6291460
  200.3 4.9 %slice-start = ((s8[8388608]{0:T(1024)(128)(4,1)}), s8[4194304]{0:T(1024)(128)(4,1)S(1)}, s32[]{:S(2)}) async-start(s8[8388608]{0:T(1024)(128)(4,1)} %bitcast.247), calls=%async_computation.7 | async-start | bytes 8388608
  202.4 3.3 %slice-start.1 = ((s8[8388608]{0:T(1024)(128)(4,1)}), s8[4194304]{0:T(1024)(128)(4,1)S(1)}, s32[]{:S(2)}) async-start(s8[8388608]{0:T(1024)(128)(4,1)} %bitcast.247), calls=%async_computation.8 | async-start | bytes 8388608
  209.5 22.1 %all-to-all-start.6 = ((bf16[8,128,128]{1,2,0:T(8,128)(2,1)}), bf16[8,128,128]{1,2,0:T(8,128)(2,1)S(1)}, u32[]{:S(2)}, u32[]{:S(2)}) async-start(bf16[8,128,128]{1,2,0:T(8,128)(2,1)} %copy.127), calls=%async_computation.6 | async-start | bytes 524288 | tf_op jit(solution)/shard_map/all_to_all | solution.py:158
  214.0 5.7 %copy-start.12 = (bf16[64,8,8,128]{3,2,1,0:T(8,128)(2,1)S(1)}, bf16[64,8,8,128]{3,2,1,0:T(8,128)(2,1)}, u32[]{:S(2)}) copy-start(bf16[64,8,8,128]{3,2,1,0:T(8,128)(2,1)} %copy-done.11) | copy-start | bytes 3145732
  220.9 5.2 %copy-start.10 = (bf16[64,8,8,128]{3,2,1,0:T(8,128)(2,1)S(1)}, bf16[64,8,8,128]{3,2,1,0:T(8,128)(2,1)}, u32[]{:S(2)}) copy-start(bf16[64,8,8,128]{3,2,1,0:T(8,128)(2,1)} %copy-done.9) | copy-start | bytes 3145732
  229.2 7.3 %copy-start.16 = (bf16[4,128,128]{2,1,0:T(8,128)(2,1)S(1)}, bf16[4,128,128]{2,1,0:T(8,128)(2,1)}, u32[]{:S(2)}) copy-start(bf16[4,128,128]{2,1,0:T(8,128)(2,1)} %slice.54) | copy-start | bytes 393220
  231.6 12.1 %all-to-all-start.5 = ((bf16[8,128,128]{2,1,0:T(8,128)(2,1)}), bf16[8,128,128]{2,1,0:T(8,128)(2,1)S(1)}, u32[]{:S(2)}, u32[]{:S(2)}) async-start(bf16[8,128,128]{2,1,0:T(8,128)(2,1)} %bitcast.71), calls=%async_computation.5 | async-start | bytes 524288 | tf_op jit(solution)/shard_map/all_to_all | solution.py:155
  243.7 31.1 %all-to-all-start.4 = ((bf16[8,128,1024]{2,1,0:T(8,128)(2,1)}), bf16[8,128,1024]{2,1,0:T(8,128)(2,1)S(1)}, u32[]{:S(2)}, u32[]{:S(2)}) async-start(bf16[8,128,1024]{2,1,0:T(8,128)(2,1)} %convert_element_type.113), calls=%async_computation.4 | async-start | bytes 4194304 | tf_op jit(solution)/shard_map/all_to_all | solution.py:154
  (3 other events, 4.6 us)
where the time goes:
time: 287 us; the launch traced here: 282 us
  blocking collectives  80 us (28%)
  local copies, waits for them, and re-layouts  52.2 us (18%)
  waiting for transfers between devices  47 us (16%)
  matrix products  36.5 us (13%)
  starting transfers between devices  34.5 us (12%)
  other arithmetic  30 us (10%)
    psum x1, blocking collectives, per_device(): totals = lax.psum(contribution, ('dp', 'ctx'))  80 us
    all_to_all x1, waiting for transfers between devices, per_device(): lax.all_to_all(grad_q, 'ctx', split_axis=0, concat_axis=1, tiled=True)  24.5 us
    unnamed x66, local copies, waits for them, and re-layouts  22.8 us
    all_to_all x1, waiting for transfers between devices, per_device(): lax.all_to_all(queries[0], 'ctx', split_axis=1, concat_axis=0, tiled=True)  15.1 us
    reduce_sum x2, other arithmetic, attend_forward(): jnp.sum(expo, axis=-1, keepdims=True)  11.5 us
    convert_element_type x2, other arithmetic, attend_forward(): (expo / jnp.sum(expo, axis=-1, keepdims=True)).astype(jnp.bfloat16)  10.3 us
    dot_general x2, matrix products, attend_forward(): jnp.einsum('qkgd,skd->kgqs', q_four[first:top], k_three[:top], preferred_...  9.31 us
    concatenate x2, local copies, waits for them, and re-layouts, attend_forward(): return (probs, jnp.concatenate(outputs, axis=0))  9.24 us
  transfers between devices with their start and end apart: 7, of which 4 were waited for; matrix products, arithmetic and copies ran while one was open for 32% of the time, Pallas kernels for 0%

commit v1 on v0

v1 whole, which is shorter than its diff:
```python
import functools

import jax
import jax.numpy as jnp
from jax import lax
from jax.experimental import pallas as pl
from jax.experimental.pallas import tpu as pltpu
from jax.sharding import PartitionSpec as P

HD = 128
SEQS = 4
GROUP = 8
BETA = 2.0
LOSS_SCALE = 1024.0
NEG_FILL = -1e30
LOG2E = 1.4426950408889634
SCALE = HD**-0.5
WINDOW = 5
CTX = 8
HEADS = (4, 4)
F32 = jnp.float32
BF16 = jnp.bfloat16
NT = (((1,), (1,)), ((), ()))
TN = (((0,), (0,)), ((), ()))
VMEM = pl.BlockSpec(memory_space=pltpu.VMEM)
SMEM = pl.BlockSpec(memory_space=pltpu.SMEM)

SIBLING = [(i, i ^ 1) for i in range(CTX)]


def shift(by):
    return [(i, i + by) for i in range(CTX) if 0 <= i + by < CTX]


def cut(at, width):
    return slice(at * width, (at + 1) * width)


def pick_row(array, row):
    rows = lax.broadcasted_iota(jnp.int32, array.shape, 0)
    return jnp.sum(jnp.where(rows == row, array, 0), axis=0, keepdims=True)


def window_bias(rank, place, seg_ref, tok):
    pack = pick_row(seg_ref[...], rank)
    mine = pick_row(seg_ref[:, pl.ds(pl.multiple_of(place * tok, tok), tok)], rank)
    start = jnp.zeros((1, tok), jnp.int32)
    for slot in range(SEQS - 1):
        count = jnp.sum((pack == slot).astype(F32)).astype(jnp.int32)
        start = start + jnp.where(mine > slot, count, 0)
    last = place * tok + lax.broadcasted_iota(jnp.int32, (1, tok), 1)
    core = lax.rem(place, 2)
    at = lax.broadcasted_iota(jnp.int32, (tok, tok), 0)
    parts = []
    for block in (place, place - 2, place - 4, place - 1 - 2 * core, place - 3 + 2 * core):
        pos = at + block * tok
        parts.append(jnp.where((pos >= start) & (pos <= last), 0.0, NEG_FILL))
    return jnp.concatenate(parts, axis=0), mine


def attend(first, heads, final, where_ref, seg_ref, term_in, q_ref, u_ref, *refs):
    tok = q_ref.shape[0]
    width = heads * HD
    blocks = refs[:WINDOW]
    dq_ref, term_ref, near_ref, far_ref, pair_ref, own_ref = refs[WINDOW:]
    bias, mine = window_bias(where_ref[0], where_ref[1], seg_ref, tok)
    bias = jnp.concatenate([bias] * GROUP, axis=1)
    term = term_in[...]
    for head in range(heads):
        keys = jnp.concatenate([ref[:, cut(head, HD)] for ref in blocks], axis=0)
        values = jnp.concatenate([ref[:, cut(heads + head, HD)] for ref in blocks], axis=0)
        base = (first + head) * GROUP
        q = jnp.concatenate([q_ref[:, cut(base + g, HD)] for g in range(GROUP)], axis=0)
        u = jnp.concatenate([u_ref[:, cut(base + g, HD)] for g in range(GROUP)], axis=0)
        scores = lax.dot_general(keys, q, NT, preferred_element_type=F32)
        scores = scores * (SCALE * LOG2E) + bias
        expo = jnp.exp2(scores - jnp.max(scores, axis=0, keepdims=True))
        probs = expo * (1.0 / jnp.sum(expo, axis=0, keepdims=True))
        dprob = lax.dot_general(values, u, NT, preferred_element_type=F32)
        delta = jnp.sum(probs * dprob, axis=0, keepdims=True)
        dscore = (probs * (dprob - delta)).astype(BF16)
        dv = jnp.dot(probs.astype(BF16), u, preferred_element_type=F32)
        dk = jnp.dot(dscore, q, preferred_element_type=F32) * SCALE
        dq = lax.dot_general(dscore, keys, TN, preferred_element_type=F32) * SCALE
        for g in range(GROUP):
            term = term + delta[:, cut(g, tok)]
            dq_ref[:, cut(head * GROUP + g, HD)] = dq[cut(g, tok)].astype(BF16)
        for side, part in ((head, dk), (heads + head, dv)):
            cols = cut(side, HD)
            own_ref[:, cols] = part[:tok]
            near_ref[:, cols] = part[cut(1, tok)].astype(BF16)
            far_ref[:, cols] = part[cut(2, tok)].astype(BF16)
            pair_ref[:, cols] = part[3 * tok :].astype(BF16)
    if final:
        lane = lax.broadcasted_iota(jnp.int32, (1, HD), 1)
        row = jnp.zeros((1, HD), F32)
        for slot in range(SEQS):
            total = jnp.sum(jnp.where(mine == slot, term, 0.0), axis=1, keepdims=True)
            row = row + jnp.where(lane == where_ref[0] * SEQS + slot, total, 0.0)
        term_ref[...] = jnp.broadcast_to(row, term_ref.shape)
    else:
        term_ref[...] = term


def attend_part(part, devices, where, segments, term, queries, upstream, blocks):
    tok = queries.shape[0]
    heads = HEADS[part]
    final = part == len(HEADS) - 1
    width = 2 * heads * HD
    shapes = [
        ((tok, heads * GROUP * HD), BF16),
        ((devices, HD) if final else (1, tok), F32),
        ((tok, width), BF16),
        ((tok, width), BF16),
        ((2 * tok, width), BF16),
        ((tok, width), F32),
    ]
    return pl.pallas_call(
        functools.partial(attend, sum(HEADS[:part]), heads, final),
        in_specs=[SMEM] + [VMEM] * (4 + WINDOW),
        out_specs=[VMEM] * len(shapes),
        out_shape=[jax.ShapeDtypeStruct(shape, dtype) for shape, dtype in shapes],
        compiler_params=pltpu.CompilerParams(vmem_limit_bytes=28 * 2**20),
        cost_estimate=pl.CostEstimate(
            flops=20 * heads * GROUP * tok * WINDOW * tok * HD,
            bytes_accessed=8 * tok * heads * GROUP * HD,
            transcendentals=heads * GROUP * tok * WINDOW * tok,
        ),
    )(where, segments, term, queries, upstream, *blocks)


def merge(where_ref, near_ref, far_ref, pair_ref, own_ref, near_out, far_out, own_out):
    tok = near_ref.shape[0]
    core = lax.rem(where_ref[1], 2).astype(F32)
    near_out[...] = (near_ref[...].astype(F32) + pair_ref[:tok].astype(F32)).astype(BF16)
    fifth = pair_ref[tok:].astype(F32)
    far_out[...] = (far_ref[...].astype(F32) + core * fifth).astype(BF16)
    own_out[...] = own_ref[...] + (1.0 - core) * fifth


def merge_part(where, near, far, pair, own):
    return pl.pallas_call(
        merge,
        in_specs=[SMEM] + [VMEM] * 4,
        out_specs=[VMEM] * 3,
        out_shape=[jax.ShapeDtypeStruct(a.shape, a.dtype) for a in (near, far, own)],
    )(where, near, far, pair, own)


def weigh(where_ref, every_ref, seg_ref, partner_ref, chosen_ref, score_ref, loss_ref):
    rank, place = where_ref[0], where_ref[1]
    packs = seg_ref.shape[0]
    lane = lax.broadcasted_iota(jnp.int32, (1, HD), 1)
    row = lax.broadcasted_iota(jnp.int32, (HD, HD), 0)
    col = lax.broadcasted_iota(jnp.int32, (HD, HD), 1)
    eye = row == col
    seg = seg_ref[...]
    counts = jnp.zeros((packs, HD), F32)
    for slot in range(SEQS):
        count = jnp.sum((seg == slot).astype(F32), axis=1, keepdims=True)
        counts = counts + jnp.where(lax.rem(lane, SEQS) == slot, count, 0.0)
    pack_of = lax.broadcasted_iota(jnp.int32, (packs, HD), 0) * SEQS
    held = (lane >= pack_of) & (lane < pack_of + SEQS)
    lengths = jnp.sum(jnp.where(held, counts, 0.0), axis=0, keepdims=True)
    totals = jnp.sum(every_ref[...], axis=0, keepdims=True)
    adjusted = totals / lengths - score_ref[...]
    adjusted_col = jnp.sum(jnp.where(eye, adjusted, 0.0), axis=1, keepdims=True)
    mate = jnp.sum(jnp.where(row == partner_ref[...], adjusted_col, 0.0), axis=0, keepdims=True)
    chosen = chosen_ref[...].astype(F32)
    sign = 2.0 * chosen - 1.0
    margin = BETA * sign * (adjusted - mate)
    softplus = jnp.maximum(-margin, 0.0) + jnp.log1p(jnp.exp(-jnp.abs(margin)))
    loss_ref[0, 0] = jnp.sum(chosen * softplus)
    weight = -sign * BETA * LOSS_SCALE / (1.0 + jnp.exp(margin)) / lengths
    mine = pick_row(seg_ref[:, pl.ds(pl.multiple_of(place * HD, HD), HD)], rank)
    mine_col = jnp.sum(jnp.where(eye, mine.astype(F32), 0.0), axis=1, keepdims=True)
    hit = col == mine_col.astype(jnp.int32) + rank * SEQS
    return jnp.sum(jnp.where(hit, weight, 0.0), axis=1, keepdims=True)


def finish(where_ref, every_ref, seg_ref, partner_ref, chosen_ref, score_ref, *refs):
    parts = len(HEADS)
    dq_refs, sides = refs[:parts], refs[parts : 4 * parts]
    out_q, out_k, out_v, loss_ref, weight_ref = refs[4 * parts :]
    step = pl.program_id(0)

    @pl.when(step == 0)
    def _():
        weight = weigh(
            where_ref, every_ref, seg_ref, partner_ref, chosen_ref, score_ref, loss_ref
        )
        weight_ref[...] = jnp.broadcast_to(weight, weight_ref.shape)
        first = 0
        for part, heads in enumerate(HEADS):
            own, near, far = sides[3 * part : 3 * part + 3]
            width = heads * HD
            for out, cols in ((out_k, slice(0, width)), (out_v, slice(width, 2 * width))):
                side = own[:, cols] + near[:, cols].astype(F32) + far[:, cols].astype(F32)
                out[:, first : first + width] = (side * weight).astype(BF16)
            first += width

    weight = weight_ref[...]
    first = 0
    for part, heads in enumerate(HEADS):

        @pl.when((step >= first) & (step < first + heads))
        def _(part=part):
            for g in range(GROUP):
                cols = cut(g, HD)
                out_q[:, cols] = (dq_refs[part][:, cols].astype(F32) * weight).astype(BF16)

        first += heads


def finish_all(where, every, segments, partner, chosen, score, grad_q, sides):
    tok = grad_q[0].shape[0]
    steps = sum(HEADS)
    wide = GROUP * HD

    def whole(array):
        return pl.BlockSpec(array.shape, lambda i: (0, 0))

    q_specs = []
    first = 0
    for heads in HEADS:
        q_specs.append(
            pl.BlockSpec(
                (tok, wide),
                lambda i, first=first, heads=heads: (0, jnp.clip(i - first, 0, heads - 1)),
            )
        )
        first += heads
    small = (every, segments, partner, chosen, score)
    flat = [array for side in sides for array in side]
    kv_shape = jax.ShapeDtypeStruct((tok, steps * HD), BF16)
    kv_spec = pl.BlockSpec(kv_shape.shape, lambda i: (0, 0))
    return pl.pallas_call(
        finish,
        grid=(steps,),
        in_specs=[SMEM] + [whole(a) for a in small] + q_specs + [whole(a) for a in flat],
        out_specs=[pl.BlockSpec((tok, wide), lambda i: (0, i)), kv_spec, kv_spec, SMEM],
        out_shape=[
            jax.ShapeDtypeStruct((tok, steps * wide), BF16),
            kv_shape,
            kv_shape,
            jax.ShapeDtypeStruct((1, 1), F32),
        ],
        scratch_shapes=[pltpu.VMEM((tok, HD), F32)],
        compiler_params=pltpu.CompilerParams(vmem_limit_bytes=28 * 2**20),
    )(where, *small, *grad_q, *flat)


def after(value, *others):
    return lax.optimization_barrier((value, *others))[0]


def per_device(queries, keys, values, upstream, token_logp, segments, partner, chosen, ref_score):
    place = lax.axis_index("ctx")
    where = jnp.stack([lax.axis_index("dp"), place]).astype(jnp.int32)
    core = place % 2
    devices = lax.axis_size("dp") * CTX
    parts = range(len(HEADS))
    edges = [sum(HEADS[:part]) * HD for part in range(len(HEADS) + 1)]

    own, near, far = [], [], []
    for part in parts:
        cols = slice(edges[part], edges[part + 1])
        block = jnp.concatenate([keys[0][:, cols], values[0][:, cols]], axis=1)
        own.append(block)
        send_near = send_far = block
        if part:
            send_near, send_far = after(block, near[-1]), after(block, far[-1])
        near.append(lax.ppermute(send_near, "ctx", shift(2)))
        far.append(lax.ppermute(send_far, "ctx", shift(4)))

    term = token_logp
    grad_q, returns = [], []
    for part in parts:
        here, there = near[part], far[part]
        if part:
            here, there, _ = lax.optimization_barrier((here, there, term))
        near_pair = lax.ppermute(here, "ctx", SIBLING)
        fifth = lax.ppermute(jnp.where(core == 0, own[part], there), "ctx", SIBLING)
        blocks = (own[part], here, there, near_pair, fifth)
        dq, term, to_near, to_far, to_pair, mine = attend_part(
            part, devices, where, segments, term, queries[0], upstream[0], blocks
        )
        grad_q.append(dq)
        pair = lax.ppermute(to_pair, "ctx", SIBLING)
        near_sum, far_sum, mine = merge_part(where, to_near, to_far, pair, mine)
        near_back = lax.ppermute(near_sum, "ctx", shift(-2))
        far_back = lax.ppermute(far_sum, "ctx", shift(-4))
        returns.append((mine, near_back, far_back))

    every = lax.all_to_all(term, ("dp", "ctx"), split_axis=0, concat_axis=0, tiled=True)
    out_q, out_k, out_v, loss = finish_all(
        where,
        every,
        segments,
        partner[None],
        chosen[None],
        ref_score[None],
        grad_q,
        returns,
    )
    return out_q[None], out_k[None], out_v[None], loss.reshape(())


def solution(mesh):
    return jax.shard_map(
        per_device,
        mesh=mesh,
        in_specs=(
            P("dp", "ctx", None),
            P("dp", "ctx", None),
            P("dp", "ctx", None),
            P("dp", "ctx", None),
            P("dp", "ctx"),
            P(),
            P(),
            P(),
            P(),
        ),
        out_specs=(P("dp", "ctx", None), P("dp", "ctx", None), P("dp", "ctx", None), P()),
        check_vma=False,
    )
```

time: 287 us -> 104 us (0.36); the launches traced: 282 us -> 104 us
  blocking collectives: 80 us -> 30.7 us
  local copies, waits for them, and re-layouts: 52.2 us -> 9.12 us
  waiting for transfers between devices: 47 us -> 6.63 us
  matrix products: 36.5 us -> 0 us
  Pallas kernels: 0 us -> 30.2 us
  other arithmetic: 30 us -> 0.25 us
  starting transfers between devices: 34.5 us -> 25.5 us
    psum x1 -> x0, blocking collectives: 80 us -> none  [per_device(): totals = lax.psum(contribution, ('dp', 'ctx'))]
    all_to_all x7 -> x0, waiting for transfers between devices: 47 us -> none  [the longest x1 24.5 us: per_device(): lax.all_to_all(grad_q, 'ctx', split_axis=0, concat_axis=1, tiled=True)]
    dot_general x12 -> x0, matrix products: 36.5 us -> none  [the longest x2 9.31 us: attend_forward(): jnp.einsum('qkgd,skd->kgqs', q_four[first:top], k_three[:top], preferred_...]
    all_to_all x7 -> x0, starting transfers between devices: 34.5 us -> none  [the longest x1 6.55 us: per_device(): lax.all_to_all(keys[0], 'ctx', split_axis=1, concat_axis=0, tiled=True)]
    all_to_all x0 -> x1, blocking collectives: none -> 30.7 us  [per_device(): lax.all_to_all(term, ('dp', 'ctx'), split_axis=0, concat_axis=0, tiled=True)]
    pallas_call x0 -> x5, Pallas kernels: none -> 30.2 us  [the longest x2 20.7 us: attend_part(): pl.pallas_call(functools.partial(attend, sum(HEADS[:part]), heads, final)...]
    ppermute x0 -> x14, starting transfers between devices: none -> 25.5 us  [the longest x2 11.1 us: per_device(): far.append(lax.ppermute(send_far, 'ctx', shift(4)))]
    reduce_sum x10 -> x0, other arithmetic: 17.2 us -> none  [the longest x2 11.5 us: attend_forward(): jnp.sum(expo, axis=-1, keepdims=True)]
  transfers between devices with their start and end apart: 7 -> 14, of which waited for: 4 -> 4; matrix products, arithmetic and copies ran while one was open for 32% -> 0% of each run, Pallas kernels for 0% -> 25%
where the time goes in v1:
time: 104 us
  blocking collectives  30.7 us (30%)
  Pallas kernels  30.2 us (29%)
  starting transfers between devices  25.5 us (25%)
  local copies, waits for them, and re-layouts  9.12 us (9%)
  waiting for transfers between devices  6.63 us (6%)
  between operations  1.06 us (1%)
    all_to_all x1, blocking collectives, per_device(): lax.all_to_all(term, ('dp', 'ctx'), split_axis=0, concat_axis=0, tiled=True)  30.7 us
    pallas_call x2, Pallas kernels, attend_part(): pl.pallas_call(functools.partial(attend, sum(HEADS[:part]), heads, final)...  20.7 us
    ppermute x2, starting transfers between devices, per_device(): far.append(lax.ppermute(send_far, 'ctx', shift(4)))  11.1 us
    unnamed x40, local copies, waits for them, and re-layouts  7.96 us
    pallas_call x2, Pallas kernels, merge_part(): pl.pallas_call(merge, in_specs=[SMEM] + [VMEM] * 4, out_specs=[VMEM] * 3,...  4.86 us
    pallas_call x1, Pallas kernels, finish_all(): pl.pallas_call(finish, grid=(steps,), in_specs=[SMEM] + [whole(a) for a i...  4.64 us
    ppermute x2, starting transfers between devices, per_device(): near.append(lax.ppermute(send_near, 'ctx', shift(2)))  3.54 us
    ppermute x2, starting transfers between devices, per_device(): fifth = lax.ppermute(jnp.where(core == 0, own[part], there), 'ctx', SIBLING)  3.06 us
  transfers between devices with their start and end apart: 14, of which 4 were waited for; matrix products, arithmetic and copies ran while one was open for 0% of the time, Pallas kernels for 25%

profile of v1, /device:TPU:1, one launch (start us, length us, event | category | flops | bytes accessed | tf_op | source)
XLA Modules:
  0.0 103.5 jit_solution(54914297019876653)
XLA Ops:
  0.7 1.2 %fusion = (bf16[128,512]{1,0:T(8,128)(2,1)S(1)}, bf16[128,512]{1,0:T(8,128)(2,1)S(1)}, bf16[128,512]{1,0:T(8,128)(2,1)S(1)}, bf16[128,512]{1,0:T(8,128)(2,1)S(1)}) fusion(bf16[128,1024]{1,0:T(8,128)(2,1)} %bitcast.26, bf16[128,1024]{1,0:T(8,128)(2,1)} %bitcast.27), kind=kLoop, calls=%fused_computation.5 | loop fusion | bytes 1048576 | tf_op jit(solution)/shard_map/slice | solution.py:268
  1.8 5.5 %collective-permute-start.1 = (bf16[128,1024]{1,0:T(8,128)(2,1)S(1)}, bf16[128,1024]{1,0:T(8,128)(2,1)S(1)}, u32[]{:S(2)}, u32[]{:S(2)}) collective-permute-start(bf16[128,1024]{1,0:T(8,128)(2,1)S(1)} %pad_maximum_fusion.refs_0_), channel_id=1, source_target_pairs={{0,4},{1,5},{2,6},{3,7},{8,12},{9,13},{10,14},{11,15},{16,20},{17,... | collective-permute-start | bytes 786440 | tf_op jit(solution)/shard_map/ppermute | solution.py:274
  7.3 2.2 %collective-permute-start = (bf16[128,1024]{1,0:T(8,128)(2,1)S(1)}, bf16[128,1024]{1,0:T(8,128)(2,1)S(1)}, u32[]{:S(2)}, u32[]{:S(2)}) collective-permute-start(bf16[128,1024]{1,0:T(8,128)(2,1)S(1)} %pad_maximum_fusion.refs_0_), channel_id=1, source_target_pairs={{0,2},{1,3},{2,4},{3,5},{4,6},{5,7},{8,10},{9,11},{10,12},{11,13},... | collective-permute-start | bytes 786440 | tf_op jit(solution)/shard_map/ppermute | solution.py:273
  9.6 2.7 %collective-permute-done.1.refs_2_ = bf16[128,1024]{1,0:T(8,128)(2,1)S(1)} collective-permute-done((bf16[128,1024]{1,0:T(8,128)(2,1)S(1)}, bf16[128,1024]{1,0:T(8,128)(2,1)S(1)}, u32[]{:S(2)}, u32[]{:S(2)}) %collective-permute-start.1) | collective-permute-done | bytes 262176 | tf_op jit(solution)/shard_map/ppermute | solution.py:274
  12.4 2.8 %collective-permute-start.3 = (bf16[128,1024]{1,0:T(8,128)(2,1)S(1)}, bf16[128,1024]{1,0:T(8,128)(2,1)S(1)}, u32[]{:S(2)}, u32[]{:S(2)}) collective-permute-start(bf16[128,1024]{1,0:T(8,128)(2,1)S(1)} %broadcast_select_fusion.1), channel_id=1, source_target_pairs={{0,1},{1,0},{2,3},{3,2},{4,5},{5,4},{6,7},{7,6},{8,9},{9,8},{10,11... | collective-permute-start | bytes 786440 | tf_op jit(solution)/shard_map/ppermute | solution.py:283
  15.2 2.8 %collective-permute-done.refs_1_ = bf16[128,1024]{1,0:T(8,128)(2,1)S(1)} collective-permute-done((bf16[128,1024]{1,0:T(8,128)(2,1)S(1)}, bf16[128,1024]{1,0:T(8,128)(2,1)S(1)}, u32[]{:S(2)}, u32[]{:S(2)}) %collective-permute-start) | collective-permute-done | bytes 262176 | tf_op jit(solution)/shard_map/ppermute | solution.py:273
  17.9 1.5 %collective-permute-start.2 = (bf16[128,1024]{1,0:T(8,128)(2,1)S(1)}, bf16[128,1024]{1,0:T(8,128)(2,1)S(1)}, u32[]{:S(2)}, u32[]{:S(2)}) collective-permute-start(bf16[128,1024]{1,0:T(8,128)(2,1)S(1)} %collective-permute-done.refs_1_), channel_id=1, source_target_pairs={{0,1},{1,0},{2,3},{3,2},{4,5},{5,4},{6,7},{7,6},{8,9},{9,8},{10,11... | collective-permute-start | bytes 786440 | tf_op jit(solution)/shard_map/ppermute | solution.py:282
  19.6 5.6 %collective-permute-start.5 = (bf16[128,1024]{1,0:T(8,128)(2,1)S(1)}, bf16[128,1024]{1,0:T(8,128)(2,1)S(1)}, u32[]{:S(2)}, u32[]{:S(2)}) collective-permute-start(bf16[128,1024]{1,0:T(8,128)(2,1)S(1)} %pad_maximum_fusion.1.refs_0_), channel_id=1, source_target_pairs={{0,4},{1,5},{2,6},{3,7},{8,12},{9,13},{10,14},{11,15},{16,20},{17,... | collective-permute-start | bytes 786440 | tf_op jit(solution)/shard_map/ppermute | solution.py:274
  25.2 1.3 %collective-permute-start.4 = (bf16[128,1024]{1,0:T(8,128)(2,1)S(1)}, bf16[128,1024]{1,0:T(8,128)(2,1)S(1)}, u32[]{:S(2)}, u32[]{:S(2)}) collective-permute-start(bf16[128,1024]{1,0:T(8,128)(2,1)S(1)} %pad_maximum_fusion.1.refs_0_), channel_id=1, source_target_pairs={{0,2},{1,3},{2,4},{3,5},{4,6},{5,7},{8,10},{9,11},{10,12},{11,13},... | collective-permute-start | bytes 786440 | tf_op jit(solution)/shard_map/ppermute | solution.py:273
  26.6 1.6 %copy-done.14 = bf16[1,128,8192]{2,1,0:T(8,128)(2,1)S(1)} copy-done((bf16[1,128,8192]{2,1,0:T(8,128)(2,1)S(1)}, bf16[1,128,8192]{2,1,0:T(8,128)(2,1)}, u32[]{:S(2)}) %copy-start.14) | copy-done | bytes 2097176
  28.1 1.6 %copy-done.16 = bf16[1,128,8192]{2,1,0:T(8,128)(2,1)S(1)} copy-done((bf16[1,128,8192]{2,1,0:T(8,128)(2,1)S(1)}, bf16[1,128,8192]{2,1,0:T(8,128)(2,1)}, u32[]{:S(2)}) %copy-start.16) | copy-done | bytes 2097176
  29.7 10.1 %shard_map.120 = (bf16[128,4096]{1,0:T(8,128)(2,1)S(1)}, f32[1,128]{1,0:T(1,128)S(1)}, bf16[128,1024]{1,0:T(8,128)(2,1)S(1)}, bf16[128,1024]{1,0:T(8,128)(2,1)S(...) custom-call(s32[2]{0:T(128)S(1)} %pad_add_fusion.where_ref, s32[32,1024]{1,0:T(8,128)S(1)} %copy-done.8, ...), custom_call_target="tpu_custom_call" | custom-call | flops 6710886400 | bytes 4194304 | tf_op jit(solution)/shard_map/pallas_call | solution.py:118
  39.9 0.7 copy-done.5
  40.7 0.4 collective-permute-start.6
  41.1 0.3 collective-permute-start.7
  41.6 0.7 collective-permute-done.6.refs_3_
  42.3 0.4 collective-permute-done.7.refs_4_
  42.7 10.6 %shard_map.121 = (bf16[128,4096]{1,0:T(8,128)(2,1)S(1)}, f32[256,128]{1,0:T(8,128)S(1)}, bf16[128,1024]{1,0:T(8,128)(2,1)S(1)}, bf16[128,1024]{1,0:T(8,128)(2,1)...) custom-call(s32[2]{0:T(128)S(1)} %pad_add_fusion.where_ref, s32[32,1024]{1,0:T(8,128)S(1)} %copy-done.8, ...), custom_call_target="tpu_custom_call" | custom-call | flops 6710886400 | bytes 4194304 | tf_op jit(solution)/shard_map/pallas_call | solution.py:118
  53.3 0.8 copy-done.1
  54.1 0.7 copy-done.6
  54.8 0.7 copy-done.7
  55.5 0.4 collective-permute-start.11
  55.9 0.8 copy-done.19
  56.7 2.4 %shard_map.122 = (bf16[128,1024]{1,0:T(8,128)(2,1)}, bf16[128,1024]{1,0:T(8,128)(2,1)}, f32[128,1024]{1,0:T(8,128)}) custom-call(s32[2]{0:T(128)} %copy-done.9, bf16[128,1024]{1,0:T(8,128)(2,1)} %copy-done.4, bf16[128,1024]{1,0:T(8,128)(2,1)} %copy-done.5, bf16[256,1024]{1,0:T(8,128)(2,1)} %copy-done.19, f32[128,1024]{1,0:T(8,128)} %copy-done), custom_call_target="tpu_custom_call" | custom-call | tf_op jit(solution)/shard_map/pallas_call | solution.py:142
  59.1 1.4 %collective-permute-start.9 = (bf16[128,1024]{1,0:T(8,128)(2,1)}, bf16[128,1024]{1,0:T(8,128)(2,1)S(1)}, u32[]{:S(2)}, u32[]{:S(2)}) collective-permute-start(bf16[128,1024]{1,0:T(8,128)(2,1)} %get-tuple-element.43), channel_id=1, source_target_pairs={{2,0},{3,1},{4,2},{5,3},{6,4},{7,5},{10,8},{11,9},{12,10},{13,11},... | collective-permute-start | bytes 786440 | tf_op jit(solution)/shard_map/ppermute | solution.py:291
  60.6 1.3 %collective-permute-start.10 = (bf16[128,1024]{1,0:T(8,128)(2,1)}, bf16[128,1024]{1,0:T(8,128)(2,1)S(1)}, u32[]{:S(2)}, u32[]{:S(2)}) collective-permute-start(bf16[128,1024]{1,0:T(8,128)(2,1)} %get-tuple-element.44), channel_id=1, source_target_pairs={{4,0},{5,1},{6,2},{7,3},{12,8},{13,9},{14,10},{15,11},{20,16},{21,... | collective-permute-start | bytes 786440 | tf_op jit(solution)/shard_map/ppermute | solution.py:292
  61.9 2.4 %shard_map.123 = (bf16[128,1024]{1,0:T(8,128)(2,1)}, bf16[128,1024]{1,0:T(8,128)(2,1)}, f32[128,1024]{1,0:T(8,128)}) custom-call(s32[2]{0:T(128)} %copy-done.9, bf16[128,1024]{1,0:T(8,128)(2,1)} %copy-done.6, bf16[128,1024]{1,0:T(8,128)(2,1)} %copy-done.7, bf16[256,1024]{1,0:T(8,128)(2,1)} %collective-permute-done.11.pair_ref, f32[128,1024]{1,0:T(8,128)} %copy-done.1), custom_call_target="tpu_custom_call" | custom-call | tf_op jit(solution)/shard_map/pallas_call | solution.py:142
  64.3 1.3 %collective-permute-start.12 = (bf16[128,1024]{1,0:T(8,128)(2,1)}, bf16[128,1024]{1,0:T(8,128)(2,1)S(1)}, u32[]{:S(2)}, u32[]{:S(2)}) collective-permute-start(bf16[128,1024]{1,0:T(8,128)(2,1)} %get-tuple-element.50), channel_id=1, source_target_pairs={{2,0},{3,1},{4,2},{5,3},{6,4},{7,5},{10,8},{11,9},{12,10},{13,11},... | collective-permute-start | bytes 786440 | tf_op jit(solution)/shard_map/ppermute | solution.py:291
  65.6 1.3 %collective-permute-start.13 = (bf16[128,1024]{1,0:T(8,128)(2,1)}, bf16[128,1024]{1,0:T(8,128)(2,1)S(1)}, u32[]{:S(2)}, u32[]{:S(2)}) collective-permute-start(bf16[128,1024]{1,0:T(8,128)(2,1)} %get-tuple-element.51), channel_id=1, source_target_pairs={{4,0},{5,1},{6,2},{7,3},{12,8},{13,9},{14,10},{15,11},{20,16},{21,... | collective-permute-start | bytes 786440 | tf_op jit(solution)/shard_map/ppermute | solution.py:292
  66.9 30.7 %all_to_all.11 = f32[256,1,128]{2,1,0:T(1,128)S(1)} all-to-all(f32[256,1,128]{2,1,0:T(1,128)S(1)} %bitcast.18), channel_id=1, replica_groups=mesh['dp'=32,'ctx'=8] {'dp','ctx'}, dimensions={0} | all-to-all | bytes 262144 | tf_op jit(solution)/shard_map/all_to_all | solution.py:295
  97.7 1.0 copy-done.3
  98.7 4.6 %shard_map.124 = (bf16[128,8192]{1,0:T(8,128)(2,1)}, bf16[128,1024]{1,0:T(8,128)(2,1)}, bf16[128,1024]{1,0:T(8,128)(2,1)}, f32[1,1]{1,0:T(1,128)}) custom-call(s32[2]{0:T(128)S(1)} %copy-done.10, f32[256,128]{1,0:T(8,128)S(1)} %bitcast.17, s32[32,1024]{1,0:T(8,128)S(1)} %copy-done.8, s32[1,128]{1,0:T(1,128)S(1)} %bitcast.19, s32[1,128]{1,0:T(1,128)S(1)} %bitcast.20, ...), custom_call_target="tpu_custom_call" | custom-call | tf_op jit(solution)/shard_map/pallas_call | solution.py:237
  (48 shorter events, 0.6 us)
Async XLA Ops:
  0.6 25.9 %copy-start.8 = (s32[32,1024]{1,0:T(8,128)S(1)}, s32[32,1024]{1,0:T(8,128)}, u32[]{:S(2)}) copy-start(s32[32,1024]{1,0:T(8,128)} %seg_ref.5) | copy-start | bytes 393220
  0.6 25.9 %copy-start.18 = (f32[1,128]{1,0:T(1,128)S(1)}, f32[1,128]{1,0:T(1,128)}, u32[]{:S(2)}) copy-start(f32[1,128]{1,0:T(1,128)} %term_in.1) | copy-start | bytes 1540
  1.8 10.5 %collective-permute-start.1 = (bf16[128,1024]{1,0:T(8,128)(2,1)S(1)}, bf16[128,1024]{1,0:T(8,128)(2,1)S(1)}, u32[]{:S(2)}, u32[]{:S(2)}) collective-permute-start(bf16[128,1024]{1,0:T(8,128)(2,1)S(1)} %pad_maximum_fusion.refs_0_), channel_id=1, source_target_pairs={{0,4},{1,5},{2,6},{3,7},{8,12},{9,13},{10,14},{11,15},{16,20},{17,... | collective-permute-start | bytes 786440 | tf_op jit(solution)/shard_map/ppermute | solution.py:274
  7.3 10.6 %collective-permute-start = (bf16[128,1024]{1,0:T(8,128)(2,1)S(1)}, bf16[128,1024]{1,0:T(8,128)(2,1)S(1)}, u32[]{:S(2)}, u32[]{:S(2)}) collective-permute-start(bf16[128,1024]{1,0:T(8,128)(2,1)S(1)} %pad_maximum_fusion.refs_0_), channel_id=1, source_target_pairs={{0,2},{1,3},{2,4},{3,5},{4,6},{5,7},{8,10},{9,11},{10,12},{11,13},... | collective-permute-start | bytes 786440 | tf_op jit(solution)/shard_map/ppermute | solution.py:273
  12.4 14.1 %collective-permute-start.3 = (bf16[128,1024]{1,0:T(8,128)(2,1)S(1)}, bf16[128,1024]{1,0:T(8,128)(2,1)S(1)}, u32[]{:S(2)}, u32[]{:S(2)}) collective-permute-start(bf16[128,1024]{1,0:T(8,128)(2,1)S(1)} %broadcast_select_fusion.1), channel_id=1, source_target_pairs={{0,1},{1,0},{2,3},{3,2},{4,5},{5,4},{6,7},{7,6},{8,9},{9,8},{10,11... | collective-permute-start | bytes 786440 | tf_op jit(solution)/shard_map/ppermute | solution.py:283
  17.9 8.6 %collective-permute-start.2 = (bf16[128,1024]{1,0:T(8,128)(2,1)S(1)}, bf16[128,1024]{1,0:T(8,128)(2,1)S(1)}, u32[]{:S(2)}, u32[]{:S(2)}) collective-permute-start(bf16[128,1024]{1,0:T(8,128)(2,1)S(1)} %collective-permute-done.refs_1_), channel_id=1, source_target_pairs={{0,1},{1,0},{2,3},{3,2},{4,5},{5,4},{6,7},{7,6},{8,9},{9,8},{10,11... | collective-permute-start | bytes 786440 | tf_op jit(solution)/shard_map/ppermute | solution.py:282
  19.6 23.1 %copy-start.9 = (s32[2]{0:T(128)}, s32[2]{0:T(128)S(1)}, u32[]{:S(2)}) copy-start(s32[2]{0:T(128)S(1)} %pad_add_fusion.where_ref) | copy-start | bytes 28
  19.6 21.0 %collective-permute-start.5 = (bf16[128,1024]{1,0:T(8,128)(2,1)S(1)}, bf16[128,1024]{1,0:T(8,128)(2,1)S(1)}, u32[]{:S(2)}, u32[]{:S(2)}) collective-permute-start(bf16[128,1024]{1,0:T(8,128)(2,1)S(1)} %pad_maximum_fusion.1.refs_0_), channel_id=1, source_target_pairs={{0,4},{1,5},{2,6},{3,7},{8,12},{9,13},{10,14},{11,15},{16,20},{17,... | collective-permute-start | bytes 786440 | tf_op jit(solution)/shard_map/ppermute | solution.py:274
  25.2 15.4 %collective-permute-start.4 = (bf16[128,1024]{1,0:T(8,128)(2,1)S(1)}, bf16[128,1024]{1,0:T(8,128)(2,1)S(1)}, u32[]{:S(2)}, u32[]{:S(2)}) collective-permute-start(bf16[128,1024]{1,0:T(8,128)(2,1)S(1)} %pad_maximum_fusion.1.refs_0_), channel_id=1, source_target_pairs={{0,2},{1,3},{2,4},{3,5},{4,6},{5,7},{8,10},{9,11},{10,12},{11,13},... | collective-permute-start | bytes 786440 | tf_op jit(solution)/shard_map/ppermute | solution.py:273
  26.5 1.6 %copy-start.14 = (bf16[1,128,8192]{2,1,0:T(8,128)(2,1)S(1)}, bf16[1,128,8192]{2,1,0:T(8,128)(2,1)}, u32[]{:S(2)}) copy-start(bf16[1,128,8192]{2,1,0:T(8,128)(2,1)} %param.9) | copy-start | bytes 6291460
  28.1 1.6 %copy-start.16 = (bf16[1,128,8192]{2,1,0:T(8,128)(2,1)S(1)}, bf16[1,128,8192]{2,1,0:T(8,128)(2,1)}, u32[]{:S(2)}) copy-start(bf16[1,128,8192]{2,1,0:T(8,128)(2,1)} %param.12) | copy-start | bytes 6291460
  29.7 13.0 %copy-start.15 = (bf16[1,128,8192]{2,1,0:T(8,128)(2,1)S(1)}, bf16[1,128,8192]{2,1,0:T(8,128)(2,1)}, u32[]{:S(2)}) copy-start(bf16[1,128,8192]{2,1,0:T(8,128)(2,1)} %param.9) | copy-start | bytes 6291460
  29.7 13.0 %copy-start.17 = (bf16[1,128,8192]{2,1,0:T(8,128)(2,1)S(1)}, bf16[1,128,8192]{2,1,0:T(8,128)(2,1)}, u32[]{:S(2)}) copy-start(bf16[1,128,8192]{2,1,0:T(8,128)(2,1)} %param.12) | copy-start | bytes 6291460
  39.9 0.7 copy-start.5
  40.6 12.7 %copy-start = (f32[128,1024]{1,0:T(8,128)}, f32[128,1024]{1,0:T(8,128)S(1)}, u32[]{:S(2)}) copy-start(f32[128,1024]{1,0:T(8,128)S(1)} %get-tuple-element.41.own_ref) | copy-start | bytes 1572868
  40.6 12.7 %copy-start.4 = (bf16[128,1024]{1,0:T(8,128)(2,1)}, bf16[128,1024]{1,0:T(8,128)(2,1)S(1)}, u32[]{:S(2)}) copy-start(bf16[128,1024]{1,0:T(8,128)(2,1)S(1)} %get-tuple-element.38.near_ref) | copy-start | bytes 786436
  40.7 1.6 %collective-permute-start.6 = (bf16[128,1024]{1,0:T(8,128)(2,1)S(1)}, bf16[128,1024]{1,0:T(8,128)(2,1)S(1)}, u32[]{:S(2)}, u32[]{:S(2)}) collective-permute-start(bf16[128,1024]{1,0:T(8,128)(2,1)S(1)} %collective-permute-done.4.refs_1_), channel_id=1, source_target_pairs={{0,1},{1,0},{2,3},{3,2},{4,5},{5,4},{6,7},{7,6},{8,9},{9,8},{10,11... | collective-permute-start | bytes 786440 | tf_op jit(solution)/shard_map/ppermute | solution.py:282
  41.1 1.6 %collective-permute-start.7 = (bf16[128,1024]{1,0:T(8,128)(2,1)S(1)}, bf16[128,1024]{1,0:T(8,128)(2,1)S(1)}, u32[]{:S(2)}, u32[]{:S(2)}) collective-permute-start(bf16[128,1024]{1,0:T(8,128)(2,1)S(1)} %broadcast_select_fusion), channel_id=1, source_target_pairs={{0,1},{1,0},{2,3},{3,2},{4,5},{5,4},{6,7},{7,6},{8,9},{9,8},{10,11... | collective-permute-start | bytes 786440 | tf_op jit(solution)/shard_map/ppermute | solution.py:283
  41.3 14.5 %collective-permute-start.8 = (bf16[256,1024]{1,0:T(8,128)(2,1)S(1)}, bf16[256,1024]{1,0:T(8,128)(2,1)S(1)}, u32[]{:S(2)}, u32[]{:S(2)}) collective-permute-start(bf16[256,1024]{1,0:T(8,128)(2,1)S(1)} %get-tuple-element.40), channel_id=1, source_target_pairs={{0,1},{1,0},{2,3},{3,2},{4,5},{5,4},{6,7},{7,6},{8,9},{9,8},{10,11... | collective-permute-start | bytes 1572872 | tf_op jit(solution)/shard_map/ppermute | solution.py:289
  53.3 0.8 copy-start.1
  55.5 42.1 %copy-start.10 = (s32[2]{0:T(128)S(1)}, s32[2]{0:T(128)}, u32[]{:S(2)}) copy-start(s32[2]{0:T(128)} %copy-done.9) | copy-start | bytes 28
  55.5 42.1 %copy-start.11 = (s32[128]{0:T(128)S(1)}, s32[128]{0:T(128)}, u32[]{:S(2)}) copy-start(s32[128]{0:T(128)} %param.15) | copy-start | bytes 1540
  55.5 42.1 %copy-start.12 = (s32[128]{0:T(128)S(1)}, s32[128]{0:T(128)}, u32[]{:S(2)}) copy-start(s32[128]{0:T(128)} %param.16) | copy-start | bytes 1540
  55.5 42.1 %copy-start.13 = (f32[128]{0:T(128)S(1)}, f32[128]{0:T(128)}, u32[]{:S(2)}) copy-start(f32[128]{0:T(128)} %param.17) | copy-start | bytes 1540
  55.5 6.4 %collective-permute-start.11 = (bf16[256,1024]{1,0:T(8,128)(2,1)}, bf16[256,1024]{1,0:T(8,128)(2,1)}, u32[]{:S(2)}, u32[]{:S(2)}) collective-permute-start(bf16[256,1024]{1,0:T(8,128)(2,1)} %get-tuple-element.47), channel_id=1, source_target_pairs={{0,1},{1,0},{2,3},{3,2},{4,5},{5,4},{6,7},{7,6},{8,9},{9,8},{10,11... | collective-permute-start | bytes 1572872 | tf_op jit(solution)/shard_map/ppermute | solution.py:289
  55.9 0.8 copy-start.19
  59.1 38.5 %copy-start.2 = (f32[128,1024]{1,0:T(8,128)S(1)}, f32[128,1024]{1,0:T(8,128)}, u32[]{:S(2)}) copy-start(f32[128,1024]{1,0:T(8,128)} %get-tuple-element.42.refs_2_) | copy-start | bytes 1572868
  59.1 38.5 %collective-permute-start.9 = (bf16[128,1024]{1,0:T(8,128)(2,1)}, bf16[128,1024]{1,0:T(8,128)(2,1)S(1)}, u32[]{:S(2)}, u32[]{:S(2)}) collective-permute-start(bf16[128,1024]{1,0:T(8,128)(2,1)} %get-tuple-element.43), channel_id=1, source_target_pairs={{2,0},{3,1},{4,2},{5,3},{6,4},{7,5},{10,8},{11,9},{12,10},{13,11},... | collective-permute-start | bytes 786440 | tf_op jit(solution)/shard_map/ppermute | solution.py:291
  60.6 37.0 %collective-permute-start.10 = (bf16[128,1024]{1,0:T(8,128)(2,1)}, bf16[128,1024]{1,0:T(8,128)(2,1)S(1)}, u32[]{:S(2)}, u32[]{:S(2)}) collective-permute-start(bf16[128,1024]{1,0:T(8,128)(2,1)} %get-tuple-element.44), channel_id=1, source_target_pairs={{4,0},{5,1},{6,2},{7,3},{12,8},{13,9},{14,10},{15,11},{20,16},{21,... | collective-permute-start | bytes 786440 | tf_op jit(solution)/shard_map/ppermute | solution.py:292
  64.3 33.3 %collective-permute-start.12 = (bf16[128,1024]{1,0:T(8,128)(2,1)}, bf16[128,1024]{1,0:T(8,128)(2,1)S(1)}, u32[]{:S(2)}, u32[]{:S(2)}) collective-permute-start(bf16[128,1024]{1,0:T(8,128)(2,1)} %get-tuple-element.50), channel_id=1, source_target_pairs={{2,0},{3,1},{4,2},{5,3},{6,4},{7,5},{10,8},{11,9},{12,10},{13,11},... | collective-permute-start | bytes 786440 | tf_op jit(solution)/shard_map/ppermute | solution.py:291
  65.6 32.0 %collective-permute-start.13 = (bf16[128,1024]{1,0:T(8,128)(2,1)}, bf16[128,1024]{1,0:T(8,128)(2,1)S(1)}, u32[]{:S(2)}, u32[]{:S(2)}) collective-permute-start(bf16[128,1024]{1,0:T(8,128)(2,1)} %get-tuple-element.51), channel_id=1, source_target_pairs={{4,0},{5,1},{6,2},{7,3},{12,8},{13,9},{14,10},{15,11},{20,16},{21,... | collective-permute-start | bytes 786440 | tf_op jit(solution)/shard_map/ppermute | solution.py:292
  97.7 1.0 %copy-start.3 = (f32[128,1024]{1,0:T(8,128)S(1)}, f32[128,1024]{1,0:T(8,128)}, u32[]{:S(2)}) copy-start(f32[128,1024]{1,0:T(8,128)} %get-tuple-element.49.refs_5_) | copy-start | bytes 1572868
  (2 other events, 1.4 us)

commit v2 on v1

v2 whole, which is shorter than its diff:
```python
import functools

import jax
import jax.numpy as jnp
from jax import lax
from jax.experimental import pallas as pl
from jax.experimental.pallas import tpu as pltpu
from jax.sharding import PartitionSpec as P

HD = 128
SEQS = 4
GROUP = 8
BETA = 2.0
LOSS_SCALE = 1024.0
NEG_FILL = -1e30
LOG2E = 1.4426950408889634
SCALE = HD**-0.5
WINDOW = 5
CTX = 8
VMEM_BYTES = 24 * 2**20
CHUNK = 2
HEADS = (4, 4)
PER_STEP = 2
F32 = jnp.float32
BF16 = jnp.bfloat16
NT = (((1,), (1,)), ((), ()))
TN = (((0,), (0,)), ((), ()))
VMEM = pl.BlockSpec(memory_space=pltpu.VMEM)
LIGHT = pl.CostEstimate(flops=1000, bytes_accessed=1000, transcendentals=0)
SMEM = pl.BlockSpec(memory_space=pltpu.SMEM)

SIBLING = [(i, i ^ 1) for i in range(CTX)]


def shift(by):
    return [(i, i + by) for i in range(CTX) if 0 <= i + by < CTX]


def cut(at, width):
    return slice(at * width, (at + 1) * width)


def pick_row(array, row):
    rows = lax.broadcasted_iota(jnp.int32, array.shape, 0)
    return jnp.sum(jnp.where(rows == row, array, 0), axis=0, keepdims=True)


def window_bias(rank, place, seg_ref, tok):
    pack = pick_row(seg_ref[...], rank)
    mine = pick_row(seg_ref[:, pl.ds(pl.multiple_of(place * tok, tok), tok)], rank)
    start = jnp.zeros((1, tok), jnp.int32)
    for slot in range(SEQS - 1):
        count = jnp.sum((pack == slot).astype(F32)).astype(jnp.int32)
        start = start + jnp.where(mine > slot, count, 0)
    last = place * tok + lax.broadcasted_iota(jnp.int32, (1, tok), 1)
    core = lax.rem(place, 2)
    at = lax.broadcasted_iota(jnp.int32, (tok, tok), 0)
    parts = []
    for block in (place, place - 2, place - 4, place - 1 - 2 * core, place - 3 + 2 * core):
        pos = at + block * tok
        parts.append(jnp.where((pos >= start) & (pos <= last), 0.0, NEG_FILL))
    return jnp.concatenate(parts, axis=0), mine


def lengths_row(seg):
    packs = seg.shape[0]
    lane = lax.broadcasted_iota(jnp.int32, (1, HD), 1)
    counts = jnp.zeros((packs, HD), F32)
    for slot in range(SEQS):
        count = jnp.sum((seg == slot).astype(F32), axis=1, keepdims=True)
        counts = counts + jnp.where(lax.rem(lane, SEQS) == slot, count, 0.0)
    pack_of = lax.broadcasted_iota(jnp.int32, (packs, HD), 0) * SEQS
    held = (lane >= pack_of) & (lane < pack_of + SEQS)
    return jnp.sum(jnp.where(held, counts, 0.0), axis=0, keepdims=True)


def stage(where_ref, seg_ref, q_ref, u_ref, bias_ref, hit_ref, length_ref, *stacks):
    tok = q_ref.shape[0]
    rank = where_ref[0]
    bias_ref[...], mine = window_bias(rank, where_ref[1], seg_ref, tok)
    length_ref[...] = lengths_row(seg_ref[...])
    row = lax.broadcasted_iota(jnp.int32, (tok, HD), 0)
    col = lax.broadcasted_iota(jnp.int32, (tok, HD), 1)
    mine = jnp.sum(jnp.where(row == col, mine.astype(F32), 0.0), axis=1, keepdims=True)
    hit_ref[...] = (col == mine.astype(jnp.int32) + rank * SEQS).astype(F32)
    parts = len(HEADS)
    for source, outs in ((q_ref, stacks[:parts]), (u_ref, stacks[parts:])):
        first = 0
        for out, heads in zip(outs, HEADS):
            for g in range(heads * GROUP):
                out[cut(g, tok), :] = source[:, cut(first + g, HD)]
            first += heads * GROUP


def window(blocks, head):
    return jnp.concatenate([ref[:, cut(head, HD)] for ref in blocks], axis=0)


def forward_chunk(keys, values, q, u, bias):
    scores = lax.dot_general(keys, q, NT, preferred_element_type=F32)
    scores = scores * (SCALE * LOG2E) + bias
    expo = jnp.exp2(scores - jnp.max(scores, axis=0, keepdims=True))
    probs = expo * (1.0 / jnp.sum(expo, axis=0, keepdims=True))
    dprob = lax.dot_general(values, u, NT, preferred_element_type=F32)
    delta = jnp.sum(probs * dprob, axis=0, keepdims=True)
    dscore = (probs * (dprob - delta)).astype(BF16)
    return probs.astype(BF16), dscore, delta


def forward_head(keys, values, q, u, bias):
    chunks = []
    for at in range(GROUP // CHUNK):
        rows = cut(at, q.shape[0] // (GROUP // CHUNK))
        chunks.append(forward_chunk(keys, values, q[rows], u[rows], bias))
    return (jnp.concatenate(side, axis=1) for side in zip(*chunks))


def backward_head(head, keys, q, u, probs, dscore, outs):
    dq_ref, near_ref, far_ref, pair_ref, own_ref = outs
    tok = near_ref.shape[1]
    dv = jnp.dot(probs, u, preferred_element_type=F32)
    dk = jnp.dot(dscore, q, preferred_element_type=F32) * SCALE
    dq = lax.dot_general(dscore, keys, TN, preferred_element_type=F32) * SCALE
    for g in range(GROUP):
        dq_ref[:, cut(head * GROUP + g, HD)] = dq[cut(g, tok)].astype(BF16)
    cols = cut(head, HD)
    for side, part in enumerate((dk, dv)):
        own_ref[side, :, cols] = part[:tok]
        near_ref[side, :, cols] = part[cut(1, tok)].astype(BF16)
        far_ref[side, :, cols] = part[cut(2, tok)].astype(BF16)
        pair_ref[0, side, :, cols] = part[cut(3, tok)].astype(BF16)
        pair_ref[1, side, :, cols] = part[cut(4, tok)].astype(BF16)


def backward_shapes(tok, heads):
    width = heads * HD
    return [
        ((tok, heads * GROUP * HD), BF16),
        ((2, tok, width), BF16),
        ((2, tok, width), BF16),
        ((2, 2, tok, width), BF16),
        ((2, tok, width), F32),
    ]


def local_call(kernel, args, shapes, cost, scalars=0):
    return pl.pallas_call(
        kernel,
        in_specs=[SMEM] * scalars + [VMEM] * (len(args) - scalars),
        out_specs=[VMEM] * len(shapes),
        out_shape=[jax.ShapeDtypeStruct(shape, dtype) for shape, dtype in shapes],
        compiler_params=pltpu.CompilerParams(vmem_limit_bytes=VMEM_BYTES),
        cost_estimate=cost,
    )(*args)


def attend(heads, final, where_ref, seg_ref, term_in, bias_ref, q_ref, u_ref, *refs):
    blocks, term_ref, outs = refs[:-6], refs[-6], refs[-5:]
    tok = bias_ref.shape[1]
    bias = jnp.concatenate([bias_ref[...]] * CHUNK, axis=1)
    term = term_in[...]
    for head in range(heads):
        keys, values = window(blocks, head), window(blocks, heads + head)
        rows = cut(head, GROUP * tok)
        q, u = q_ref[rows, :], u_ref[rows, :]
        probs, dscore, delta = forward_head(keys, values, q, u, bias)
        for g in range(GROUP):
            term = term + delta[:, cut(g, tok)]
        backward_head(head, keys, q, u, probs, dscore, outs)
    if final:
        rank, place = where_ref[0], where_ref[1]
        mine = pick_row(seg_ref[:, pl.ds(pl.multiple_of(place * tok, tok), tok)], rank)
        lane = lax.broadcasted_iota(jnp.int32, (1, HD), 1)
        row = jnp.zeros((1, HD), F32)
        for slot in range(SEQS):
            total = jnp.sum(jnp.where(mine == slot, term, 0.0), axis=1, keepdims=True)
            row = row + jnp.where(lane == rank * SEQS + slot, total, 0.0)
        term_ref[...] = jnp.broadcast_to(row, term_ref.shape)
    else:
        term_ref[...] = term


def merge(where_ref, *refs):
    near_out, far_out = refs[-2:]
    core = lax.rem(where_ref[1], 2).astype(F32)
    first = 0
    for part, heads in enumerate(HEADS):
        near, far, pair = refs[3 * part : 3 * part + 3]
        cols = slice(first, first + heads * HD)
        near_out[:, :, cols] = (near[...].astype(F32) + pair[0].astype(F32)).astype(BF16)
        far_out[:, :, cols] = (far[...].astype(F32) + core * pair[1].astype(F32)).astype(BF16)
        first += heads * HD


def weigh(every_ref, length_ref, hit_ref, partner_ref, chosen_ref, score_ref, loss_ref):
    row = lax.broadcasted_iota(jnp.int32, (HD, HD), 0)
    col = lax.broadcasted_iota(jnp.int32, (HD, HD), 1)
    lengths = length_ref[...]
    totals = jnp.sum(every_ref[...], axis=0, keepdims=True)
    adjusted = totals / lengths - score_ref[...]
    adjusted_col = jnp.sum(jnp.where(row == col, adjusted, 0.0), axis=1, keepdims=True)
    mate = jnp.sum(jnp.where(row == partner_ref[...], adjusted_col, 0.0), axis=0, keepdims=True)
    chosen = chosen_ref[...].astype(F32)
    sign = 2.0 * chosen - 1.0
    margin = BETA * sign * (adjusted - mate)
    softplus = jnp.maximum(-margin, 0.0) + jnp.log1p(jnp.exp(-jnp.abs(margin)))
    loss_ref[0, 0] = jnp.sum(chosen * softplus)
    weight = -sign * BETA * LOSS_SCALE / (1.0 + jnp.exp(margin)) / lengths
    return jnp.sum(hit_ref[...] * weight, axis=1, keepdims=True)


def finish(where_ref, *refs):
    small, refs = refs[:6], refs[6:]
    parts = len(HEADS)
    dq_refs, own_refs, pair_refs = (refs[i * parts : (i + 1) * parts] for i in range(3))
    near, far, out_q, out_k, out_v, loss_ref, weight_ref = refs[3 * parts :]
    step = pl.program_id(0)

    @pl.when(step == 0)
    def _():
        weight = weigh(*small, loss_ref)
        weight_ref[...] = jnp.broadcast_to(weight, weight_ref.shape)

    weight = weight_ref[...]
    even = 1.0 - lax.rem(where_ref[1], 2).astype(F32)
    origin = [(part, head) for part, heads in enumerate(HEADS) for head in range(heads)]
    for at in range(len(origin) // PER_STEP):

        @pl.when(step == at)
        def _(at=at):
            for here in range(PER_STEP):
                part, local = origin[at * PER_STEP + here]
                cols, back = cut(local, HD), cut(at * PER_STEP + here, HD)
                for out, base in ((out_k, 0), (out_v, 1)):
                    side = own_refs[part][base, :, cols]
                    side = side + even * pair_refs[part][1, base, :, cols].astype(F32)
                    side = side + near[base, :, back].astype(F32)
                    side = side + far[base, :, back].astype(F32)
                    out[:, cut(here, HD)] = (side * weight).astype(BF16)
                for g in range(GROUP):
                    dq = dq_refs[part][:, cut(local * GROUP + g, HD)].astype(F32)
                    out_q[:, cut(here * GROUP + g, HD)] = (dq * weight).astype(BF16)


def finish_all(where, small, grad_q, mines, pairs, backs):
    tok = grad_q[0].shape[0]
    steps = sum(HEADS) // PER_STEP
    arrays = [*small, *grad_q, *mines, *pairs, *backs]
    widths = [PER_STEP * GROUP * HD, PER_STEP * HD, PER_STEP * HD]
    return pl.pallas_call(
        finish,
        grid=(steps,),
        in_specs=[SMEM] + [VMEM] * len(arrays),
        out_specs=[pl.BlockSpec((tok, width), lambda i: (0, i)) for width in widths] + [SMEM],
        out_shape=[jax.ShapeDtypeStruct((tok, steps * width), BF16) for width in widths]
        + [jax.ShapeDtypeStruct((1, 1), F32)],
        scratch_shapes=[pltpu.VMEM((tok, HD), F32)],
        compiler_params=pltpu.CompilerParams(vmem_limit_bytes=VMEM_BYTES),
    )(where, *arrays)


def gather_window(own, near, far, core, halves):
    pairs = [near, jnp.where(core == 0, own, far)]
    if halves:
        half = near.shape[0] // 2
        pairs = [array[rows] for array in pairs for rows in (slice(0, half), slice(half, None))]
    pairs = [lax.ppermute(array, "ctx", SIBLING) for array in pairs]
    return (own, near, far, *pairs)


def tie(value, *others):
    return lax.optimization_barrier((value, *others))[0]


def per_device(queries, keys, values, upstream, token_logp, segments, partner, chosen, ref_score):
    place = lax.axis_index("ctx")
    where = jnp.stack([lax.axis_index("dp"), place]).astype(jnp.int32)
    core = place % 2
    tok = queries.shape[1]
    devices = lax.axis_size("dp") * CTX
    own, near, far = [], [], []
    first = 0
    for heads in HEADS:
        cols = slice(first * HD, (first + heads) * HD)
        block = jnp.concatenate([keys[0][:, cols], values[0][:, cols]], axis=1)
        own.append(block)
        near.append(lax.ppermute(block, "ctx", shift(2)))
        far.append(lax.ppermute(block, "ctx", shift(4)))
        first += heads
    parts = len(HEADS)
    bias, hit, lengths, *stacks = local_call(
        stage,
        (where, segments, queries[0], upstream[0]),
        [((WINDOW * tok, tok), F32), ((tok, HD), F32), ((1, HD), F32)]
        + [((heads * GROUP * tok, HD), BF16) for heads in HEADS] * 2,
        None,
        1,
    )

    term = token_logp
    grad_q, mines, pairs, outward = [], [], [], []
    for part, heads in enumerate(HEADS):
        final = part == len(HEADS) - 1
        ready = term if part else bias
        here, there, _ = lax.optimization_barrier((near[part], far[part], ready))
        blocks = gather_window(own[part], here, there, core, part == 0)
        term, dq, to_near, to_far, to_pair, mine = local_call(
            functools.partial(attend, heads, final),
            (where, segments, term, bias, stacks[part], stacks[parts + part], *blocks),
            [((devices, HD) if final else (1, tok), F32)] + backward_shapes(tok, heads),
            LIGHT,
            1,
        )
        grad_q.append(dq)
        mines.append(mine)
        pairs.append(lax.ppermute(to_pair, "ctx", SIBLING))
        outward += [to_near, to_far, pairs[-1]]
    shape = ((2, tok, sum(HEADS) * HD), BF16)
    near_sum, far_sum = local_call(merge, (where, *outward), [shape] * 2, LIGHT, 1)
    backs = (
        lax.ppermute(near_sum, "ctx", shift(-2)),
        lax.ppermute(far_sum, "ctx", shift(-4)),
    )

    term = tie(term, near_sum, far_sum)
    every = lax.all_to_all(term, ("dp", "ctx"), split_axis=0, concat_axis=0, tiled=True)
    small = (every, lengths, hit, partner[None], chosen[None], ref_score[None])
    out_q, out_k, out_v, loss = finish_all(where, small, grad_q, mines, pairs, backs)
    return out_q[None], out_k[None], out_v[None], loss.reshape(())


def solution(mesh):
    return jax.shard_map(
        per_device,
        mesh=mesh,
        in_specs=(
            P("dp", "ctx", None),
            P("dp", "ctx", None),
            P("dp", "ctx", None),
            P("dp", "ctx", None),
            P("dp", "ctx"),
            P(),
            P(),
            P(),
            P(),
        ),
        out_specs=(P("dp", "ctx", None), P("dp", "ctx", None), P("dp", "ctx", None), P()),
        check_vma=False,
    )
```

time: 104 us -> 83.7 us (0.80)
  starting transfers between devices: 25.5 us -> 18.1 us
  local copies, waits for them, and re-layouts: 9.12 us -> 3.87 us
  Pallas kernels: 30.2 us -> 25.8 us
  waiting for transfers between devices: 6.63 us -> 4.16 us
    ppermute x14, starting transfers between devices: 25.5 us -> 18.1 us  [the longest x2 5.95 us: per_device(): near.append(lax.ppermute(block, 'ctx', shift(2)))]
    unnamed x40 -> x26, local copies, waits for them, and re-layouts: 7.96 us -> 2.55 us
    pallas_call x5, Pallas kernels: 30.2 us -> 25.8 us  [the longest x4 22.4 us: local_call(): pl.pallas_call(kernel, in_specs=[SMEM] * scalars + [VMEM] * (len(args) -...]
    ppermute x14, waiting for transfers between devices: 6.63 us -> 4.16 us  [the longest x6 2.6 us: gather_window(): pairs = [lax.ppermute(array, 'ctx', SIBLING) for array in pairs]]
  transfers between devices with their start and end apart: 14 -> 14, of which waited for: 4 -> 6; matrix products, arithmetic and copies ran while one was open for 0% -> 0% of each run, Pallas kernels for 25% -> 26%
where the time goes in v2:
time: 83.7 us; the launch traced here: 83.4 us
  blocking collectives  30.3 us (36%)
  Pallas kernels  25.8 us (31%)
  starting transfers between devices  18.1 us (22%)
  waiting for transfers between devices  4.16 us (5%)
  local copies, waits for them, and re-layouts  3.87 us (5%)
  between operations  0.92 us (1%)
    all_to_all x1, blocking collectives, per_device(): lax.all_to_all(term, ('dp', 'ctx'), split_axis=0, concat_axis=0, tiled=True)  30.3 us
    pallas_call x4, Pallas kernels, local_call(): pl.pallas_call(kernel, in_specs=[SMEM] * scalars + [VMEM] * (len(args) -...  22.4 us
    ppermute x2, starting transfers between devices, per_device(): near.append(lax.ppermute(block, 'ctx', shift(2)))  5.95 us
    ppermute x2, starting transfers between devices, per_device(): far.append(lax.ppermute(block, 'ctx', shift(4)))  5.65 us
    pallas_call x1, Pallas kernels, finish_all(): pl.pallas_call(finish, grid=(steps,), in_specs=[SMEM] + [VMEM] * len(arra...  3.36 us
    ppermute x6, starting transfers between devices, gather_window(): pairs = [lax.ppermute(array, 'ctx', SIBLING) for array in pairs]  3.13 us
    ppermute x6, waiting for transfers between devices, gather_window(): pairs = [lax.ppermute(array, 'ctx', SIBLING) for array in pairs]  2.6 us
    unnamed x26, local copies, waits for them, and re-layouts  2.55 us
  transfers between devices with their start and end apart: 14, of which 6 were waited for; matrix products, arithmetic and copies ran while one was open for 0% of the time, Pallas kernels for 26%

profile of v2, /device:TPU:1, one launch (start us, length us, event | category | flops | bytes accessed | tf_op | source)
XLA Modules:
  0.0 83.4 jit_solution(10757274995254562257)
XLA Ops:
  0.6 1.3 %fusion = (bf16[128,512]{1,0:T(8,128)(2,1)S(1)}, bf16[128,512]{1,0:T(8,128)(2,1)S(1)}, bf16[128,512]{1,0:T(8,128)(2,1)S(1)}, bf16[128,512]{1,0:T(8,128)(2,1)S(1)}) fusion(bf16[128,1024]{1,0:T(8,128)(2,1)} %bitcast.24, bf16[128,1024]{1,0:T(8,128)(2,1)} %bitcast.25), kind=kLoop, calls=%fused_computation.5 | loop fusion | bytes 1048576 | tf_op jit(solution)/shard_map/slice | solution.py:285
  2.0 4.0 %collective-permute-start = (bf16[128,1024]{1,0:T(8,128)(2,1)S(1)}, bf16[128,1024]{1,0:T(8,128)(2,1)S(1)}, u32[]{:S(2)}, u32[]{:S(2)}) collective-permute-start(bf16[128,1024]{1,0:T(8,128)(2,1)S(1)} %pad_maximum_fusion.refs_0_), channel_id=1, source_target_pairs={{0,2},{1,3},{2,4},{3,5},{4,6},{5,7},{8,10},{9,11},{10,12},{11,13},... | collective-permute-start | bytes 786440 | tf_op jit(solution)/shard_map/ppermute | solution.py:287
  6.0 4.4 %collective-permute-start.1 = (bf16[128,1024]{1,0:T(8,128)(2,1)S(1)}, bf16[128,1024]{1,0:T(8,128)(2,1)S(1)}, u32[]{:S(2)}, u32[]{:S(2)}) collective-permute-start(bf16[128,1024]{1,0:T(8,128)(2,1)S(1)} %pad_maximum_fusion.refs_0_), channel_id=1, source_target_pairs={{0,4},{1,5},{2,6},{3,7},{8,12},{9,13},{10,14},{11,15},{16,20},{17,... | collective-permute-start | bytes 786440 | tf_op jit(solution)/shard_map/ppermute | solution.py:288
  10.4 2.0 %collective-permute-start.6 = (bf16[128,1024]{1,0:T(8,128)(2,1)S(1)}, bf16[128,1024]{1,0:T(8,128)(2,1)}, u32[]{:S(2)}, u32[]{:S(2)}) collective-permute-start(bf16[128,1024]{1,0:T(8,128)(2,1)S(1)} %pad_maximum_fusion.1.refs_0_), channel_id=1, source_target_pairs={{0,2},{1,3},{2,4},{3,5},{4,6},{5,7},{8,10},{9,11},{10,12},{11,13},... | collective-permute-start | bytes 786440 | tf_op jit(solution)/shard_map/ppermute | solution.py:287
  12.4 1.3 %collective-permute-start.7 = (bf16[128,1024]{1,0:T(8,128)(2,1)S(1)}, bf16[128,1024]{1,0:T(8,128)(2,1)S(1)}, u32[]{:S(2)}, u32[]{:S(2)}) collective-permute-start(bf16[128,1024]{1,0:T(8,128)(2,1)S(1)} %pad_maximum_fusion.1.refs_0_), channel_id=1, source_target_pairs={{0,4},{1,5},{2,6},{3,7},{8,12},{9,13},{10,14},{11,15},{16,20},{17,... | collective-permute-start | bytes 786440 | tf_op jit(solution)/shard_map/ppermute | solution.py:288
  13.7 0.1 pad_add_fusion.where_ref
  13.8 1.6 %copy-done.1 = bf16[1,128,8192]{2,1,0:T(8,128)(2,1)S(1)} copy-done((bf16[1,128,8192]{2,1,0:T(8,128)(2,1)S(1)}, bf16[1,128,8192]{2,1,0:T(8,128)(2,1)}, u32[]{:S(2)}) %copy-start.1) | copy-done | bytes 2097176
  15.4 0.9 %copy-done.2 = s32[32,1024]{1,0:T(8,128)S(1)} copy-done((s32[32,1024]{1,0:T(8,128)S(1)}, s32[32,1024]{1,0:T(8,128)}, u32[]{:S(2)}) %copy-start.2) | copy-done | bytes 131096
  16.3 1.4 %shard_map.120 = (f32[640,128]{1,0:T(8,128)S(1)}, f32[128,128]{1,0:T(8,128)S(1)}, f32[1,128]{1,0:T(1,128)S(1)}, bf16[4096,128]{1,0:T(8,128)(2,1)S(1)}, bf16[4096...) custom-call(s32[2]{0:T(128)S(1)} %pad_add_fusion.where_ref, ...), custom_call_target="tpu_custom_call" | custom-call | tf_op jit(solution)/shard_map/pallas_call | solution.py:147
  17.8 0.1 broadcast_select_fusion.1
  17.9 1.6 %collective-permute-start.4 = (bf16[64,1024]{1,0:T(8,128)(2,1)S(1)}, bf16[64,1024]{1,0:T(8,128)(2,1)S(1)}, u32[]{:S(2)}, u32[]{:S(2)}) collective-permute-start(bf16[64,1024]{1,0:T(8,128)(2,1)S(1)} %get-tuple-element.69), channel_id=1, source_target_pairs={{0,1},{1,0},{2,3},{3,2},{4,5},{5,4},{6,7},{7,6},{8,9},{9,8},{10,11... | collective-permute-start | bytes 393224 | tf_op jit(solution)/shard_map/ppermute | solution.py:267
  19.4 0.1 collective-permute-start.5
  19.6 0.5 collective-permute-start.2
  20.1 0.4 collective-permute-done.4.refs_5_
  20.4 0.4 collective-permute-start.3
  20.8 0.3 collective-permute-done.2.refs_3_
  21.0 0.7 collective-permute-done.3.refs_4_
  21.8 9.9 %shard_map.121 = (f32[1,128]{1,0:T(1,128)S(1)}, bf16[128,4096]{1,0:T(8,128)(2,1)S(1)}, bf16[2,128,512]{2,1,0:T(8,128)(2,1)S(1)}, bf16[2,128,512]{2,1,0:T(8,128)(...) custom-call(s32[2]{0:T(128)S(1)} %pad_add_fusion.where_ref, s32[32,1024]{1,0:T(8,128)S(1)} %copy-done.2, ...), custom_call_target="tpu_custom_call" | custom-call | flops 1000 | bytes 1000 | tf_op jit(solution)/shard_map/pallas_call | solution.py:147
  31.7 0.1 broadcast_select_fusion
  31.8 0.4 collective-permute-start.9
  32.2 0.1 collective-permute-start.8
  32.4 0.4 collective-permute-start.10
  32.8 0.7 collective-permute-done.9.refs_4_
  33.4 0.6 collective-permute-done.8.refs_3_
  34.0 10.2 %shard_map.122 = (f32[256,128]{1,0:T(8,128)S(1)}, bf16[128,4096]{1,0:T(8,128)(2,1)S(1)}, bf16[2,128,512]{2,1,0:T(8,128)(2,1)S(1)}, bf16[2,128,512]{2,1,0:T(8,128...) custom-call(s32[2]{0:T(128)S(1)} %pad_add_fusion.where_ref, s32[32,1024]{1,0:T(8,128)S(1)} %copy-done.2, ...), custom_call_target="tpu_custom_call" | custom-call | flops 1000 | bytes 1000 | tf_op jit(solution)/shard_map/pallas_call | solution.py:147
  44.3 0.4 collective-permute-start.11
  44.7 1.5 %collective-permute-done.11.refs_5_.refs_11_ = bf16[2,2,128,512]{3,2,1,0:T(8,128)(2,1)S(1)} collective-permute-done((bf16[2,2,128,512]{3,2,1,0:T(8,128)(2,1)S(1)}, bf16[2,2,128,512]{3,2,1,0:T(8,128)(2,1)S(1)}, u32[]{:S(2)}, u32[]{:S(2)}) %collective-permute-start.11) | collective-permute-done | bytes 524320 | tf_op jit(solution)/shard_map/ppermute | solution.py:316
  46.3 0.8 %shard_map.123 = (bf16[2,128,1024]{2,1,0:T(8,128)(2,1)S(1)}, bf16[2,128,1024]{2,1,0:T(8,128)(2,1)S(1)}) custom-call(s32[2]{0:T(128)S(1)} %pad_add_fusion.where_ref, bf16[2,128,512]{2,1,0:T(8,128)(2,1)S(1)} %get-tuple-element.45.refs_0_, bf16[2,128,512]{2,1,0:T(8,128)(2,1)S(1)} %get-tuple-element.46.refs_1_, ...), custom_call_target="tpu_custom_call" | custom-call | flops 1000 | bytes 1000 | tf_op jit(solution)/shard_map/pallas_call | solution.py:147
  47.1 1.3 %collective-permute-start.12 = (bf16[2,128,1024]{2,1,0:T(8,128)(2,1)S(1)}, bf16[2,128,1024]{2,1,0:T(8,128)(2,1)S(1)}, u32[]{:S(2)}, u32[]{:S(2)}) collective-permute-start(bf16[2,128,1024]{2,1,0:T(8,128)(2,1)S(1)} %get-tuple-element.51), channel_id=1, source_target_pairs={{2,0},{3,1},{4,2},{5,3},{6,4},{7,5},{10,8},{11,9},{12,10},{13,11},... | collective-permute-start | bytes 1572872 | tf_op jit(solution)/shard_map/ppermute | solution.py:321
  48.4 1.3 %collective-permute-start.13 = (bf16[2,128,1024]{2,1,0:T(8,128)(2,1)S(1)}, bf16[2,128,1024]{2,1,0:T(8,128)(2,1)S(1)}, u32[]{:S(2)}, u32[]{:S(2)}) collective-permute-start(bf16[2,128,1024]{2,1,0:T(8,128)(2,1)S(1)} %get-tuple-element.52), channel_id=1, source_target_pairs={{4,0},{5,1},{6,2},{7,3},{12,8},{13,9},{14,10},{15,11},{20,16},{21,... | collective-permute-start | bytes 1572872 | tf_op jit(solution)/shard_map/ppermute | solution.py:322
  49.7 30.3 %all_to_all.11 = f32[256,1,128]{2,1,0:T(1,128)S(1)} all-to-all(f32[256,1,128]{2,1,0:T(1,128)S(1)} %bitcast.20), channel_id=1, replica_groups=mesh['dp'=32,'ctx'=8] {'dp','ctx'}, dimensions={0} | all-to-all | bytes 262144 | tf_op jit(solution)/shard_map/all_to_all | solution.py:326
  80.0 3.4 %shard_map.124 = (bf16[128,8192]{1,0:T(8,128)(2,1)}, bf16[128,1024]{1,0:T(8,128)(2,1)}, bf16[128,1024]{1,0:T(8,128)(2,1)}, f32[1,1]{1,0:T(1,128)}) custom-call(s32[2]{0:T(128)S(1)} %pad_add_fusion.where_ref, f32[256,128]{1,0:T(8,128)S(1)} %bitcast.19, f32[1,128]{1,0:T(1,128)S(1)} %get-tuple-element.54.refs_1_, f32[128,128]{1,0:T(8,128)S(1)} %get-tuple-element.55.refs_2_, ...), custom_call_target="tpu_custom_call" | custom-call | tf_op jit(solution)/shard_map/pallas_call | solution.py:250
  (36 shorter events, 0.2 us)
Async XLA Ops:
  0.6 13.1 %copy-start = (bf16[1,128,8192]{2,1,0:T(8,128)(2,1)S(1)}, bf16[1,128,8192]{2,1,0:T(8,128)(2,1)}, u32[]{:S(2)}) copy-start(bf16[1,128,8192]{2,1,0:T(8,128)(2,1)} %param.9) | copy-start | bytes 6291460
  1.9 8.4 %copy-start.9 = (bf16[128,512]{1,0:T(8,128)(2,1)}, bf16[128,512]{1,0:T(8,128)(2,1)S(1)}, u32[]{:S(2)}) copy-start(bf16[128,512]{1,0:T(8,128)(2,1)S(1)} %get-tuple-element.65) | copy-start | bytes 393220
  1.9 8.4 %copy-start.11 = (bf16[128,512]{1,0:T(8,128)(2,1)}, bf16[128,512]{1,0:T(8,128)(2,1)S(1)}, u32[]{:S(2)}) copy-start(bf16[128,512]{1,0:T(8,128)(2,1)S(1)} %get-tuple-element.72) | copy-start | bytes 393220
  1.9 8.4 %copy-start.7 = (bf16[128,512]{1,0:T(8,128)(2,1)}, bf16[128,512]{1,0:T(8,128)(2,1)S(1)}, u32[]{:S(2)}) copy-start(bf16[128,512]{1,0:T(8,128)(2,1)S(1)} %get-tuple-element.73) | copy-start | bytes 393220
  2.0 15.7 %collective-permute-start = (bf16[128,1024]{1,0:T(8,128)(2,1)S(1)}, bf16[128,1024]{1,0:T(8,128)(2,1)S(1)}, u32[]{:S(2)}, u32[]{:S(2)}) collective-permute-start(bf16[128,1024]{1,0:T(8,128)(2,1)S(1)} %pad_maximum_fusion.refs_0_), channel_id=1, source_target_pairs={{0,2},{1,3},{2,4},{3,5},{4,6},{5,7},{8,10},{9,11},{10,12},{11,13},... | collective-permute-start | bytes 786440 | tf_op jit(solution)/shard_map/ppermute | solution.py:287
  6.0 11.8 %collective-permute-start.1 = (bf16[128,1024]{1,0:T(8,128)(2,1)S(1)}, bf16[128,1024]{1,0:T(8,128)(2,1)S(1)}, u32[]{:S(2)}, u32[]{:S(2)}) collective-permute-start(bf16[128,1024]{1,0:T(8,128)(2,1)S(1)} %pad_maximum_fusion.refs_0_), channel_id=1, source_target_pairs={{0,4},{1,5},{2,6},{3,7},{8,12},{9,13},{10,14},{11,15},{16,20},{17,... | collective-permute-start | bytes 786440 | tf_op jit(solution)/shard_map/ppermute | solution.py:288
  10.4 21.3 %collective-permute-start.6 = (bf16[128,1024]{1,0:T(8,128)(2,1)S(1)}, bf16[128,1024]{1,0:T(8,128)(2,1)}, u32[]{:S(2)}, u32[]{:S(2)}) collective-permute-start(bf16[128,1024]{1,0:T(8,128)(2,1)S(1)} %pad_maximum_fusion.1.refs_0_), channel_id=1, source_target_pairs={{0,2},{1,3},{2,4},{3,5},{4,6},{5,7},{8,10},{9,11},{10,12},{11,13},... | collective-permute-start | bytes 786440 | tf_op jit(solution)/shard_map/ppermute | solution.py:287
  12.4 19.3 %collective-permute-start.7 = (bf16[128,1024]{1,0:T(8,128)(2,1)S(1)}, bf16[128,1024]{1,0:T(8,128)(2,1)S(1)}, u32[]{:S(2)}, u32[]{:S(2)}) collective-permute-start(bf16[128,1024]{1,0:T(8,128)(2,1)S(1)} %pad_maximum_fusion.1.refs_0_), channel_id=1, source_target_pairs={{0,4},{1,5},{2,6},{3,7},{8,12},{9,13},{10,14},{11,15},{16,20},{17,... | collective-permute-start | bytes 786440 | tf_op jit(solution)/shard_map/ppermute | solution.py:288
  13.8 1.6 %copy-start.1 = (bf16[1,128,8192]{2,1,0:T(8,128)(2,1)S(1)}, bf16[1,128,8192]{2,1,0:T(8,128)(2,1)}, u32[]{:S(2)}) copy-start(bf16[1,128,8192]{2,1,0:T(8,128)(2,1)} %param.12) | copy-start | bytes 6291460
  15.4 0.9 %copy-start.2 = (s32[32,1024]{1,0:T(8,128)S(1)}, s32[32,1024]{1,0:T(8,128)}, u32[]{:S(2)}) copy-start(s32[32,1024]{1,0:T(8,128)} %seg_ref.5) | copy-start | bytes 393220
  16.3 1.5 %copy-start.10 = (bf16[128,512]{1,0:T(8,128)(2,1)S(1)}, bf16[128,512]{1,0:T(8,128)(2,1)}, u32[]{:S(2)}) copy-start(bf16[128,512]{1,0:T(8,128)(2,1)} %copy-done.9) | copy-start | bytes 393220
  16.3 1.5 %copy-start.12 = (bf16[128,512]{1,0:T(8,128)(2,1)S(1)}, bf16[128,512]{1,0:T(8,128)(2,1)}, u32[]{:S(2)}) copy-start(bf16[128,512]{1,0:T(8,128)(2,1)} %copy-done.11) | copy-start | bytes 393220
  16.3 5.5 %copy-start.3 = (f32[1,128]{1,0:T(1,128)S(1)}, f32[1,128]{1,0:T(1,128)}, u32[]{:S(2)}) copy-start(f32[1,128]{1,0:T(1,128)} %term_in.1) | copy-start | bytes 1540
  17.9 2.6 %collective-permute-start.4 = (bf16[64,1024]{1,0:T(8,128)(2,1)S(1)}, bf16[64,1024]{1,0:T(8,128)(2,1)S(1)}, u32[]{:S(2)}, u32[]{:S(2)}) collective-permute-start(bf16[64,1024]{1,0:T(8,128)(2,1)S(1)} %get-tuple-element.69), channel_id=1, source_target_pairs={{0,1},{1,0},{2,3},{3,2},{4,5},{5,4},{6,7},{7,6},{8,9},{9,8},{10,11... | collective-permute-start | bytes 393224 | tf_op jit(solution)/shard_map/ppermute | solution.py:267
  19.4 12.3 %copy-start.8 = (bf16[128,512]{1,0:T(8,128)(2,1)S(1)}, bf16[128,512]{1,0:T(8,128)(2,1)}, u32[]{:S(2)}) copy-start(bf16[128,512]{1,0:T(8,128)(2,1)} %copy-done.7) | copy-start | bytes 393220
  19.4 1.4 %collective-permute-start.5 = (bf16[64,1024]{1,0:T(8,128)(2,1)S(1)}, bf16[64,1024]{1,0:T(8,128)(2,1)S(1)}, u32[]{:S(2)}, u32[]{:S(2)}) collective-permute-start(bf16[64,1024]{1,0:T(8,128)(2,1)S(1)} %get-tuple-element.68), channel_id=1, source_target_pairs={{0,1},{1,0},{2,3},{3,2},{4,5},{5,4},{6,7},{7,6},{8,9},{9,8},{10,11... | collective-permute-start | bytes 393224 | tf_op jit(solution)/shard_map/ppermute | solution.py:267
  19.6 1.5 %collective-permute-start.2 = (bf16[64,1024]{1,0:T(8,128)(2,1)S(1)}, bf16[64,1024]{1,0:T(8,128)(2,1)S(1)}, u32[]{:S(2)}, u32[]{:S(2)}) collective-permute-start(bf16[64,1024]{1,0:T(8,128)(2,1)S(1)} %get-tuple-element.71), channel_id=1, source_target_pairs={{0,1},{1,0},{2,3},{3,2},{4,5},{5,4},{6,7},{7,6},{8,9},{9,8},{10,11... | collective-permute-start | bytes 393224 | tf_op jit(solution)/shard_map/ppermute | solution.py:267
  20.4 1.3 %collective-permute-start.3 = (bf16[64,1024]{1,0:T(8,128)(2,1)S(1)}, bf16[64,1024]{1,0:T(8,128)(2,1)S(1)}, u32[]{:S(2)}, u32[]{:S(2)}) collective-permute-start(bf16[64,1024]{1,0:T(8,128)(2,1)S(1)} %get-tuple-element.70), channel_id=1, source_target_pairs={{0,1},{1,0},{2,3},{3,2},{4,5},{5,4},{6,7},{7,6},{8,9},{9,8},{10,11... | collective-permute-start | bytes 393224 | tf_op jit(solution)/shard_map/ppermute | solution.py:267
  31.8 1.6 %collective-permute-start.9 = (bf16[128,1024]{1,0:T(8,128)(2,1)S(1)}, bf16[128,1024]{1,0:T(8,128)(2,1)S(1)}, u32[]{:S(2)}, u32[]{:S(2)}) collective-permute-start(bf16[128,1024]{1,0:T(8,128)(2,1)S(1)} %broadcast_select_fusion), channel_id=1, source_target_pairs={{0,1},{1,0},{2,3},{3,2},{4,5},{5,4},{6,7},{7,6},{8,9},{9,8},{10,11... | collective-permute-start | bytes 786440 | tf_op jit(solution)/shard_map/ppermute | solution.py:267
  32.2 1.8 %collective-permute-start.8 = (bf16[128,1024]{1,0:T(8,128)(2,1)}, bf16[128,1024]{1,0:T(8,128)(2,1)S(1)}, u32[]{:S(2)}, u32[]{:S(2)}) collective-permute-start(bf16[128,1024]{1,0:T(8,128)(2,1)} %collective-permute-done.6.refs_1_), channel_id=1, source_target_pairs={{0,1},{1,0},{2,3},{3,2},{4,5},{5,4},{6,7},{7,6},{8,9},{9,8},{10,11... | collective-permute-start | bytes 786440 | tf_op jit(solution)/shard_map/ppermute | solution.py:267
  32.4 12.3 %collective-permute-start.10 = (bf16[2,2,128,512]{3,2,1,0:T(8,128)(2,1)S(1)}, bf16[2,2,128,512]{3,2,1,0:T(8,128)(2,1)S(1)}, u32[]{:S(2)}, u32[]{:S(2)}) collective-permute-start(bf16[2,2,128,512]{3,2,1,0:T(8,128)(2,1)S(1)} %get-tuple-element.47), channel_id=1, source_target_pairs={{0,1},{1,0},{2,3},{3,2},{4,5},{5,4},{6,7},{7,6},{8,9},{9,8},{10,11... | collective-permute-start | bytes 1572872 | tf_op jit(solution)/shard_map/ppermute | solution.py:316
  44.3 35.7 %copy-start.4 = (s32[128]{0:T(128)S(1)}, s32[128]{0:T(128)}, u32[]{:S(2)}) copy-start(s32[128]{0:T(128)} %param.15) | copy-start | bytes 1540
  44.3 35.7 %copy-start.5 = (s32[128]{0:T(128)S(1)}, s32[128]{0:T(128)}, u32[]{:S(2)}) copy-start(s32[128]{0:T(128)} %param.16) | copy-start | bytes 1540
  44.3 35.7 %copy-start.6 = (f32[128]{0:T(128)S(1)}, f32[128]{0:T(128)}, u32[]{:S(2)}) copy-start(f32[128]{0:T(128)} %param.17) | copy-start | bytes 1540
  44.3 2.0 %collective-permute-start.11 = (bf16[2,2,128,512]{3,2,1,0:T(8,128)(2,1)S(1)}, bf16[2,2,128,512]{3,2,1,0:T(8,128)(2,1)S(1)}, u32[]{:S(2)}, u32[]{:S(2)}) collective-permute-start(bf16[2,2,128,512]{3,2,1,0:T(8,128)(2,1)S(1)} %get-tuple-element.50), channel_id=1, source_target_pairs={{0,1},{1,0},{2,3},{3,2},{4,5},{5,4},{6,7},{7,6},{8,9},{9,8},{10,11... | collective-permute-start | bytes 1572872 | tf_op jit(solution)/shard_map/ppermute | solution.py:316
  47.1 32.9 %collective-permute-start.12 = (bf16[2,128,1024]{2,1,0:T(8,128)(2,1)S(1)}, bf16[2,128,1024]{2,1,0:T(8,128)(2,1)S(1)}, u32[]{:S(2)}, u32[]{:S(2)}) collective-permute-start(bf16[2,128,1024]{2,1,0:T(8,128)(2,1)S(1)} %get-tuple-element.51), channel_id=1, source_target_pairs={{2,0},{3,1},{4,2},{5,3},{6,4},{7,5},{10,8},{11,9},{12,10},{13,11},... | collective-permute-start | bytes 1572872 | tf_op jit(solution)/shard_map/ppermute | solution.py:321
  48.4 31.6 %collective-permute-start.13 = (bf16[2,128,1024]{2,1,0:T(8,128)(2,1)S(1)}, bf16[2,128,1024]{2,1,0:T(8,128)(2,1)S(1)}, u32[]{:S(2)}, u32[]{:S(2)}) collective-permute-start(bf16[2,128,1024]{2,1,0:T(8,128)(2,1)S(1)} %get-tuple-element.52), channel_id=1, source_target_pairs={{4,0},{5,1},{6,2},{7,3},{12,8},{13,9},{14,10},{15,11},{20,16},{21,... | collective-permute-start | bytes 1572872 | tf_op jit(solution)/shard_map/ppermute | solution.py:322

commit v3 on v2

--- a/solution.py
+++ b/solution.py
@@ -20,7 +20,7 @@
 VMEM_BYTES = 24 * 2**20
 CHUNK = 2
 HEADS = (4, 4)
-PER_STEP = 2
+PER_STEP = 4
 F32 = jnp.float32
 BF16 = jnp.bfloat16
 NT = (((1,), (1,)), ((), ()))
@@ -100,11 +100,11 @@
     scores = lax.dot_general(keys, q, NT, preferred_element_type=F32)
     scores = scores * (SCALE * LOG2E) + bias
     expo = jnp.exp2(scores - jnp.max(scores, axis=0, keepdims=True))
-    probs = expo * (1.0 / jnp.sum(expo, axis=0, keepdims=True))
+    share = 1.0 / jnp.sum(expo, axis=0, keepdims=True)
+    probs = expo.astype(BF16) * share.astype(BF16)
     dprob = lax.dot_general(values, u, NT, preferred_element_type=F32)
-    delta = jnp.sum(probs * dprob, axis=0, keepdims=True)
-    dscore = (probs * (dprob - delta)).astype(BF16)
-    return probs.astype(BF16), dscore, delta
+    delta = jnp.sum(expo * dprob, axis=0, keepdims=True) * share
+    return probs, probs * (dprob - delta).astype(BF16), delta
 
 
 def forward_head(keys, values, q, u, bias):

time: 83.7 us -> 82.1 us (0.981)
  Pallas kernels: 25.8 us -> 24.2 us
    pallas_call x4, Pallas kernels: 22.4 us -> 21.3 us  [local_call(): pl.pallas_call(kernel, in_specs=[SMEM] * scalars + [VMEM] * (len(args) -...]
  transfers between devices with their start and end apart: 14 -> 14, of which waited for: 6 -> 6; matrix products, arithmetic and copies ran while one was open for 0% -> 0% of each run, Pallas kernels for 26% -> 25%
where the time goes in v3:
time: 82.1 us; the launch traced here: 81.7 us
  blocking collectives  30.3 us (37%)
  Pallas kernels  24.2 us (29%)
  starting transfers between devices  18.1 us (22%)
  waiting for transfers between devices  4.17 us (5%)
  local copies, waits for them, and re-layouts  3.87 us (5%)
  between operations  0.92 us (1%)
    all_to_all x1, blocking collectives, per_device(): lax.all_to_all(term, ('dp', 'ctx'), split_axis=0, concat_axis=0, tiled=True)  30.3 us
    pallas_call x4, Pallas kernels, local_call(): pl.pallas_call(kernel, in_specs=[SMEM] * scalars + [VMEM] * (len(args) -...  21.3 us
    ppermute x2, starting transfers between devices, per_device(): near.append(lax.ppermute(block, 'ctx', shift(2)))  5.95 us
    ppermute x2, starting transfers between devices, per_device(): far.append(lax.ppermute(block, 'ctx', shift(4)))  5.65 us
    ppermute x6, starting transfers between devices, gather_window(): pairs = [lax.ppermute(array, 'ctx', SIBLING) for array in pairs]  3.13 us
    pallas_call x1, Pallas kernels, finish_all(): pl.pallas_call(finish, grid=(steps,), in_specs=[SMEM] + [VMEM] * len(arra...  2.91 us
    ppermute x6, waiting for transfers between devices, gather_window(): pairs = [lax.ppermute(array, 'ctx', SIBLING) for array in pairs]  2.6 us
    unnamed x26, local copies, waits for them, and re-layouts  2.55 us
  transfers between devices with their start and end apart: 14, of which 6 were waited for; matrix products, arithmetic and copies ran while one was open for 0% of the time, Pallas kernels for 25%

profile of v3, /device:TPU:1, one launch (start us, length us, event | category | flops | bytes accessed | tf_op | source)
XLA Modules:
  0.0 81.7 jit_solution(13793795107083077607)
XLA Ops:
  0.6 1.3 %fusion = (bf16[128,512]{1,0:T(8,128)(2,1)S(1)}, bf16[128,512]{1,0:T(8,128)(2,1)S(1)}, bf16[128,512]{1,0:T(8,128)(2,1)S(1)}, bf16[128,512]{1,0:T(8,128)(2,1)S(1)}) fusion(bf16[128,1024]{1,0:T(8,128)(2,1)} %bitcast.24, bf16[128,1024]{1,0:T(8,128)(2,1)} %bitcast.25), kind=kLoop, calls=%fused_computation.5 | loop fusion | bytes 1048576 | tf_op jit(solution)/shard_map/slice | solution.py:285
  2.0 4.0 %collective-permute-start = (bf16[128,1024]{1,0:T(8,128)(2,1)S(1)}, bf16[128,1024]{1,0:T(8,128)(2,1)S(1)}, u32[]{:S(2)}, u32[]{:S(2)}) collective-permute-start(bf16[128,1024]{1,0:T(8,128)(2,1)S(1)} %pad_maximum_fusion.refs_0_), channel_id=1, source_target_pairs={{0,2},{1,3},{2,4},{3,5},{4,6},{5,7},{8,10},{9,11},{10,12},{11,13},... | collective-permute-start | bytes 786440 | tf_op jit(solution)/shard_map/ppermute | solution.py:287
  6.0 4.4 %collective-permute-start.1 = (bf16[128,1024]{1,0:T(8,128)(2,1)S(1)}, bf16[128,1024]{1,0:T(8,128)(2,1)S(1)}, u32[]{:S(2)}, u32[]{:S(2)}) collective-permute-start(bf16[128,1024]{1,0:T(8,128)(2,1)S(1)} %pad_maximum_fusion.refs_0_), channel_id=1, source_target_pairs={{0,4},{1,5},{2,6},{3,7},{8,12},{9,13},{10,14},{11,15},{16,20},{17,... | collective-permute-start | bytes 786440 | tf_op jit(solution)/shard_map/ppermute | solution.py:288
  10.4 2.0 %collective-permute-start.6 = (bf16[128,1024]{1,0:T(8,128)(2,1)S(1)}, bf16[128,1024]{1,0:T(8,128)(2,1)}, u32[]{:S(2)}, u32[]{:S(2)}) collective-permute-start(bf16[128,1024]{1,0:T(8,128)(2,1)S(1)} %pad_maximum_fusion.1.refs_0_), channel_id=1, source_target_pairs={{0,2},{1,3},{2,4},{3,5},{4,6},{5,7},{8,10},{9,11},{10,12},{11,13},... | collective-permute-start | bytes 786440 | tf_op jit(solution)/shard_map/ppermute | solution.py:287
  12.4 1.3 %collective-permute-start.7 = (bf16[128,1024]{1,0:T(8,128)(2,1)S(1)}, bf16[128,1024]{1,0:T(8,128)(2,1)S(1)}, u32[]{:S(2)}, u32[]{:S(2)}) collective-permute-start(bf16[128,1024]{1,0:T(8,128)(2,1)S(1)} %pad_maximum_fusion.1.refs_0_), channel_id=1, source_target_pairs={{0,4},{1,5},{2,6},{3,7},{8,12},{9,13},{10,14},{11,15},{16,20},{17,... | collective-permute-start | bytes 786440 | tf_op jit(solution)/shard_map/ppermute | solution.py:288
  13.7 0.1 pad_add_fusion.where_ref
  13.8 1.6 %copy-done.1 = bf16[1,128,8192]{2,1,0:T(8,128)(2,1)S(1)} copy-done((bf16[1,128,8192]{2,1,0:T(8,128)(2,1)S(1)}, bf16[1,128,8192]{2,1,0:T(8,128)(2,1)}, u32[]{:S(2)}) %copy-start.1) | copy-done | bytes 2097176
  15.4 0.9 %copy-done.2 = s32[32,1024]{1,0:T(8,128)S(1)} copy-done((s32[32,1024]{1,0:T(8,128)S(1)}, s32[32,1024]{1,0:T(8,128)}, u32[]{:S(2)}) %copy-start.2) | copy-done | bytes 131096
  16.3 1.4 %shard_map.120 = (f32[640,128]{1,0:T(8,128)S(1)}, f32[128,128]{1,0:T(8,128)S(1)}, f32[1,128]{1,0:T(1,128)S(1)}, bf16[4096,128]{1,0:T(8,128)(2,1)S(1)}, bf16[4096...) custom-call(s32[2]{0:T(128)S(1)} %pad_add_fusion.where_ref, ...), custom_call_target="tpu_custom_call" | custom-call | tf_op jit(solution)/shard_map/pallas_call | solution.py:147
  17.8 0.1 broadcast_select_fusion.1
  17.9 1.6 %collective-permute-start.4 = (bf16[64,1024]{1,0:T(8,128)(2,1)S(1)}, bf16[64,1024]{1,0:T(8,128)(2,1)S(1)}, u32[]{:S(2)}, u32[]{:S(2)}) collective-permute-start(bf16[64,1024]{1,0:T(8,128)(2,1)S(1)} %get-tuple-element.69), channel_id=1, source_target_pairs={{0,1},{1,0},{2,3},{3,2},{4,5},{5,4},{6,7},{7,6},{8,9},{9,8},{10,11... | collective-permute-start | bytes 393224 | tf_op jit(solution)/shard_map/ppermute | solution.py:267
  19.4 0.1 collective-permute-start.5
  19.6 0.5 collective-permute-start.2
  20.1 0.4 collective-permute-done.4.refs_5_
  20.4 0.4 collective-permute-start.3
  20.8 0.3 collective-permute-done.2.refs_3_
  21.0 0.7 collective-permute-done.3.refs_4_
  21.8 9.3 %shard_map.121 = (f32[1,128]{1,0:T(1,128)S(1)}, bf16[128,4096]{1,0:T(8,128)(2,1)S(1)}, bf16[2,128,512]{2,1,0:T(8,128)(2,1)S(1)}, bf16[2,128,512]{2,1,0:T(8,128)(...) custom-call(s32[2]{0:T(128)S(1)} %pad_add_fusion.where_ref, s32[32,1024]{1,0:T(8,128)S(1)} %copy-done.2, ...), custom_call_target="tpu_custom_call" | custom-call | flops 1000 | bytes 1000 | tf_op jit(solution)/shard_map/pallas_call | solution.py:147
  31.1 0.1 broadcast_select_fusion
  31.2 0.4 collective-permute-start.9
  31.6 0.2 collective-permute-start.8
  31.8 0.4 collective-permute-start.10
  32.1 0.7 collective-permute-done.9.refs_4_
  32.8 0.6 collective-permute-done.8.refs_3_
  33.4 9.7 %shard_map.122 = (f32[256,128]{1,0:T(8,128)S(1)}, bf16[128,4096]{1,0:T(8,128)(2,1)S(1)}, bf16[2,128,512]{2,1,0:T(8,128)(2,1)S(1)}, bf16[2,128,512]{2,1,0:T(8,128...) custom-call(s32[2]{0:T(128)S(1)} %pad_add_fusion.where_ref, s32[32,1024]{1,0:T(8,128)S(1)} %copy-done.2, ...), custom_call_target="tpu_custom_call" | custom-call | flops 1000 | bytes 1000 | tf_op jit(solution)/shard_map/pallas_call | solution.py:147
  43.1 0.4 collective-permute-start.11
  43.5 1.6 %collective-permute-done.11.refs_5_.refs_11_ = bf16[2,2,128,512]{3,2,1,0:T(8,128)(2,1)S(1)} collective-permute-done((bf16[2,2,128,512]{3,2,1,0:T(8,128)(2,1)S(1)}, bf16[2,2,128,512]{3,2,1,0:T(8,128)(2,1)S(1)}, u32[]{:S(2)}, u32[]{:S(2)}) %collective-permute-start.11) | collective-permute-done | bytes 524320 | tf_op jit(solution)/shard_map/ppermute | solution.py:316
  45.1 0.8 %shard_map.123 = (bf16[2,128,1024]{2,1,0:T(8,128)(2,1)S(1)}, bf16[2,128,1024]{2,1,0:T(8,128)(2,1)S(1)}) custom-call(s32[2]{0:T(128)S(1)} %pad_add_fusion.where_ref, bf16[2,128,512]{2,1,0:T(8,128)(2,1)S(1)} %get-tuple-element.45.refs_0_, bf16[2,128,512]{2,1,0:T(8,128)(2,1)S(1)} %get-tuple-element.46.refs_1_, ...), custom_call_target="tpu_custom_call" | custom-call | flops 1000 | bytes 1000 | tf_op jit(solution)/shard_map/pallas_call | solution.py:147
  45.9 1.3 %collective-permute-start.12 = (bf16[2,128,1024]{2,1,0:T(8,128)(2,1)S(1)}, bf16[2,128,1024]{2,1,0:T(8,128)(2,1)S(1)}, u32[]{:S(2)}, u32[]{:S(2)}) collective-permute-start(bf16[2,128,1024]{2,1,0:T(8,128)(2,1)S(1)} %get-tuple-element.51), channel_id=1, source_target_pairs={{2,0},{3,1},{4,2},{5,3},{6,4},{7,5},{10,8},{11,9},{12,10},{13,11},... | collective-permute-start | bytes 1572872 | tf_op jit(solution)/shard_map/ppermute | solution.py:321
  47.2 1.3 %collective-permute-start.13 = (bf16[2,128,1024]{2,1,0:T(8,128)(2,1)S(1)}, bf16[2,128,1024]{2,1,0:T(8,128)(2,1)S(1)}, u32[]{:S(2)}, u32[]{:S(2)}) collective-permute-start(bf16[2,128,1024]{2,1,0:T(8,128)(2,1)S(1)} %get-tuple-element.52), channel_id=1, source_target_pairs={{4,0},{5,1},{6,2},{7,3},{12,8},{13,9},{14,10},{15,11},{20,16},{21,... | collective-permute-start | bytes 1572872 | tf_op jit(solution)/shard_map/ppermute | solution.py:322
  48.5 30.3 %all_to_all.11 = f32[256,1,128]{2,1,0:T(1,128)S(1)} all-to-all(f32[256,1,128]{2,1,0:T(1,128)S(1)} %bitcast.20), channel_id=1, replica_groups=mesh['dp'=32,'ctx'=8] {'dp','ctx'}, dimensions={0} | all-to-all | bytes 262144 | tf_op jit(solution)/shard_map/all_to_all | solution.py:326
  78.8 2.9 %shard_map.124 = (bf16[128,8192]{1,0:T(8,128)(2,1)}, bf16[128,1024]{1,0:T(8,128)(2,1)}, bf16[128,1024]{1,0:T(8,128)(2,1)}, f32[1,1]{1,0:T(1,128)}) custom-call(s32[2]{0:T(128)S(1)} %pad_add_fusion.where_ref, f32[256,128]{1,0:T(8,128)S(1)} %bitcast.19, f32[1,128]{1,0:T(1,128)S(1)} %get-tuple-element.54.refs_1_, f32[128,128]{1,0:T(8,128)S(1)} %get-tuple-element.55.refs_2_, ...), custom_call_target="tpu_custom_call" | custom-call | tf_op jit(solution)/shard_map/pallas_call | solution.py:250
  (36 shorter events, 0.2 us)
Async XLA Ops:
  0.6 13.1 %copy-start = (bf16[1,128,8192]{2,1,0:T(8,128)(2,1)S(1)}, bf16[1,128,8192]{2,1,0:T(8,128)(2,1)}, u32[]{:S(2)}) copy-start(bf16[1,128,8192]{2,1,0:T(8,128)(2,1)} %param.9) | copy-start | bytes 6291460
  1.9 8.4 %copy-start.9 = (bf16[128,512]{1,0:T(8,128)(2,1)}, bf16[128,512]{1,0:T(8,128)(2,1)S(1)}, u32[]{:S(2)}) copy-start(bf16[128,512]{1,0:T(8,128)(2,1)S(1)} %get-tuple-element.65) | copy-start | bytes 393220
  1.9 8.4 %copy-start.11 = (bf16[128,512]{1,0:T(8,128)(2,1)}, bf16[128,512]{1,0:T(8,128)(2,1)S(1)}, u32[]{:S(2)}) copy-start(bf16[128,512]{1,0:T(8,128)(2,1)S(1)} %get-tuple-element.72) | copy-start | bytes 393220
  1.9 8.4 %copy-start.7 = (bf16[128,512]{1,0:T(8,128)(2,1)}, bf16[128,512]{1,0:T(8,128)(2,1)S(1)}, u32[]{:S(2)}) copy-start(bf16[128,512]{1,0:T(8,128)(2,1)S(1)} %get-tuple-element.73) | copy-start | bytes 393220
  2.0 15.7 %collective-permute-start = (bf16[128,1024]{1,0:T(8,128)(2,1)S(1)}, bf16[128,1024]{1,0:T(8,128)(2,1)S(1)}, u32[]{:S(2)}, u32[]{:S(2)}) collective-permute-start(bf16[128,1024]{1,0:T(8,128)(2,1)S(1)} %pad_maximum_fusion.refs_0_), channel_id=1, source_target_pairs={{0,2},{1,3},{2,4},{3,5},{4,6},{5,7},{8,10},{9,11},{10,12},{11,13},... | collective-permute-start | bytes 786440 | tf_op jit(solution)/shard_map/ppermute | solution.py:287
  6.0 11.8 %collective-permute-start.1 = (bf16[128,1024]{1,0:T(8,128)(2,1)S(1)}, bf16[128,1024]{1,0:T(8,128)(2,1)S(1)}, u32[]{:S(2)}, u32[]{:S(2)}) collective-permute-start(bf16[128,1024]{1,0:T(8,128)(2,1)S(1)} %pad_maximum_fusion.refs_0_), channel_id=1, source_target_pairs={{0,4},{1,5},{2,6},{3,7},{8,12},{9,13},{10,14},{11,15},{16,20},{17,... | collective-permute-start | bytes 786440 | tf_op jit(solution)/shard_map/ppermute | solution.py:288
  10.4 20.7 %collective-permute-start.6 = (bf16[128,1024]{1,0:T(8,128)(2,1)S(1)}, bf16[128,1024]{1,0:T(8,128)(2,1)}, u32[]{:S(2)}, u32[]{:S(2)}) collective-permute-start(bf16[128,1024]{1,0:T(8,128)(2,1)S(1)} %pad_maximum_fusion.1.refs_0_), channel_id=1, source_target_pairs={{0,2},{1,3},{2,4},{3,5},{4,6},{5,7},{8,10},{9,11},{10,12},{11,13},... | collective-permute-start | bytes 786440 | tf_op jit(solution)/shard_map/ppermute | solution.py:287
  12.4 18.7 %collective-permute-start.7 = (bf16[128,1024]{1,0:T(8,128)(2,1)S(1)}, bf16[128,1024]{1,0:T(8,128)(2,1)S(1)}, u32[]{:S(2)}, u32[]{:S(2)}) collective-permute-start(bf16[128,1024]{1,0:T(8,128)(2,1)S(1)} %pad_maximum_fusion.1.refs_0_), channel_id=1, source_target_pairs={{0,4},{1,5},{2,6},{3,7},{8,12},{9,13},{10,14},{11,15},{16,20},{17,... | collective-permute-start | bytes 786440 | tf_op jit(solution)/shard_map/ppermute | solution.py:288
  13.8 1.6 %copy-start.1 = (bf16[1,128,8192]{2,1,0:T(8,128)(2,1)S(1)}, bf16[1,128,8192]{2,1,0:T(8,128)(2,1)}, u32[]{:S(2)}) copy-start(bf16[1,128,8192]{2,1,0:T(8,128)(2,1)} %param.12) | copy-start | bytes 6291460
  15.4 0.9 %copy-start.2 = (s32[32,1024]{1,0:T(8,128)S(1)}, s32[32,1024]{1,0:T(8,128)}, u32[]{:S(2)}) copy-start(s32[32,1024]{1,0:T(8,128)} %seg_ref.5) | copy-start | bytes 393220
  16.3 1.5 %copy-start.10 = (bf16[128,512]{1,0:T(8,128)(2,1)S(1)}, bf16[128,512]{1,0:T(8,128)(2,1)}, u32[]{:S(2)}) copy-start(bf16[128,512]{1,0:T(8,128)(2,1)} %copy-done.9) | copy-start | bytes 393220
  16.3 1.5 %copy-start.12 = (bf16[128,512]{1,0:T(8,128)(2,1)S(1)}, bf16[128,512]{1,0:T(8,128)(2,1)}, u32[]{:S(2)}) copy-start(bf16[128,512]{1,0:T(8,128)(2,1)} %copy-done.11) | copy-start | bytes 393220
  16.3 5.5 %copy-start.3 = (f32[1,128]{1,0:T(1,128)S(1)}, f32[1,128]{1,0:T(1,128)}, u32[]{:S(2)}) copy-start(f32[1,128]{1,0:T(1,128)} %term_in.1) | copy-start | bytes 1540
  17.9 2.6 %collective-permute-start.4 = (bf16[64,1024]{1,0:T(8,128)(2,1)S(1)}, bf16[64,1024]{1,0:T(8,128)(2,1)S(1)}, u32[]{:S(2)}, u32[]{:S(2)}) collective-permute-start(bf16[64,1024]{1,0:T(8,128)(2,1)S(1)} %get-tuple-element.69), channel_id=1, source_target_pairs={{0,1},{1,0},{2,3},{3,2},{4,5},{5,4},{6,7},{7,6},{8,9},{9,8},{10,11... | collective-permute-start | bytes 393224 | tf_op jit(solution)/shard_map/ppermute | solution.py:267
  19.4 11.7 %copy-start.8 = (bf16[128,512]{1,0:T(8,128)(2,1)S(1)}, bf16[128,512]{1,0:T(8,128)(2,1)}, u32[]{:S(2)}) copy-start(bf16[128,512]{1,0:T(8,128)(2,1)} %copy-done.7) | copy-start | bytes 393220
  19.4 1.4 %collective-permute-start.5 = (bf16[64,1024]{1,0:T(8,128)(2,1)S(1)}, bf16[64,1024]{1,0:T(8,128)(2,1)S(1)}, u32[]{:S(2)}, u32[]{:S(2)}) collective-permute-start(bf16[64,1024]{1,0:T(8,128)(2,1)S(1)} %get-tuple-element.68), channel_id=1, source_target_pairs={{0,1},{1,0},{2,3},{3,2},{4,5},{5,4},{6,7},{7,6},{8,9},{9,8},{10,11... | collective-permute-start | bytes 393224 | tf_op jit(solution)/shard_map/ppermute | solution.py:267
  19.6 1.5 %collective-permute-start.2 = (bf16[64,1024]{1,0:T(8,128)(2,1)S(1)}, bf16[64,1024]{1,0:T(8,128)(2,1)S(1)}, u32[]{:S(2)}, u32[]{:S(2)}) collective-permute-start(bf16[64,1024]{1,0:T(8,128)(2,1)S(1)} %get-tuple-element.71), channel_id=1, source_target_pairs={{0,1},{1,0},{2,3},{3,2},{4,5},{5,4},{6,7},{7,6},{8,9},{9,8},{10,11... | collective-permute-start | bytes 393224 | tf_op jit(solution)/shard_map/ppermute | solution.py:267
  20.4 1.3 %collective-permute-start.3 = (bf16[64,1024]{1,0:T(8,128)(2,1)S(1)}, bf16[64,1024]{1,0:T(8,128)(2,1)S(1)}, u32[]{:S(2)}, u32[]{:S(2)}) collective-permute-start(bf16[64,1024]{1,0:T(8,128)(2,1)S(1)} %get-tuple-element.70), channel_id=1, source_target_pairs={{0,1},{1,0},{2,3},{3,2},{4,5},{5,4},{6,7},{7,6},{8,9},{9,8},{10,11... | collective-permute-start | bytes 393224 | tf_op jit(solution)/shard_map/ppermute | solution.py:267
  31.2 1.6 %collective-permute-start.9 = (bf16[128,1024]{1,0:T(8,128)(2,1)S(1)}, bf16[128,1024]{1,0:T(8,128)(2,1)S(1)}, u32[]{:S(2)}, u32[]{:S(2)}) collective-permute-start(bf16[128,1024]{1,0:T(8,128)(2,1)S(1)} %broadcast_select_fusion), channel_id=1, source_target_pairs={{0,1},{1,0},{2,3},{3,2},{4,5},{5,4},{6,7},{7,6},{8,9},{9,8},{10,11... | collective-permute-start | bytes 786440 | tf_op jit(solution)/shard_map/ppermute | solution.py:267
  31.6 1.8 %collective-permute-start.8 = (bf16[128,1024]{1,0:T(8,128)(2,1)}, bf16[128,1024]{1,0:T(8,128)(2,1)S(1)}, u32[]{:S(2)}, u32[]{:S(2)}) collective-permute-start(bf16[128,1024]{1,0:T(8,128)(2,1)} %collective-permute-done.6.refs_1_), channel_id=1, source_target_pairs={{0,1},{1,0},{2,3},{3,2},{4,5},{5,4},{6,7},{7,6},{8,9},{9,8},{10,11... | collective-permute-start | bytes 786440 | tf_op jit(solution)/shard_map/ppermute | solution.py:267
  31.8 11.8 %collective-permute-start.10 = (bf16[2,2,128,512]{3,2,1,0:T(8,128)(2,1)S(1)}, bf16[2,2,128,512]{3,2,1,0:T(8,128)(2,1)S(1)}, u32[]{:S(2)}, u32[]{:S(2)}) collective-permute-start(bf16[2,2,128,512]{3,2,1,0:T(8,128)(2,1)S(1)} %get-tuple-element.47), channel_id=1, source_target_pairs={{0,1},{1,0},{2,3},{3,2},{4,5},{5,4},{6,7},{7,6},{8,9},{9,8},{10,11... | collective-permute-start | bytes 1572872 | tf_op jit(solution)/shard_map/ppermute | solution.py:316
  43.1 35.7 %copy-start.4 = (s32[128]{0:T(128)S(1)}, s32[128]{0:T(128)}, u32[]{:S(2)}) copy-start(s32[128]{0:T(128)} %param.15) | copy-start | bytes 1540
  43.1 35.7 %copy-start.5 = (s32[128]{0:T(128)S(1)}, s32[128]{0:T(128)}, u32[]{:S(2)}) copy-start(s32[128]{0:T(128)} %param.16) | copy-start | bytes 1540
  43.1 35.7 %copy-start.6 = (f32[128]{0:T(128)S(1)}, f32[128]{0:T(128)}, u32[]{:S(2)}) copy-start(f32[128]{0:T(128)} %param.17) | copy-start | bytes 1540
  43.1 2.0 %collective-permute-start.11 = (bf16[2,2,128,512]{3,2,1,0:T(8,128)(2,1)S(1)}, bf16[2,2,128,512]{3,2,1,0:T(8,128)(2,1)S(1)}, u32[]{:S(2)}, u32[]{:S(2)}) collective-permute-start(bf16[2,2,128,512]{3,2,1,0:T(8,128)(2,1)S(1)} %get-tuple-element.50), channel_id=1, source_target_pairs={{0,1},{1,0},{2,3},{3,2},{4,5},{5,4},{6,7},{7,6},{8,9},{9,8},{10,11... | collective-permute-start | bytes 1572872 | tf_op jit(solution)/shard_map/ppermute | solution.py:316
  45.9 32.9 %collective-permute-start.12 = (bf16[2,128,1024]{2,1,0:T(8,128)(2,1)S(1)}, bf16[2,128,1024]{2,1,0:T(8,128)(2,1)S(1)}, u32[]{:S(2)}, u32[]{:S(2)}) collective-permute-start(bf16[2,128,1024]{2,1,0:T(8,128)(2,1)S(1)} %get-tuple-element.51), channel_id=1, source_target_pairs={{2,0},{3,1},{4,2},{5,3},{6,4},{7,5},{10,8},{11,9},{12,10},{13,11},... | collective-permute-start | bytes 1572872 | tf_op jit(solution)/shard_map/ppermute | solution.py:321
  47.2 31.6 %collective-permute-start.13 = (bf16[2,128,1024]{2,1,0:T(8,128)(2,1)S(1)}, bf16[2,128,1024]{2,1,0:T(8,128)(2,1)S(1)}, u32[]{:S(2)}, u32[]{:S(2)}) collective-permute-start(bf16[2,128,1024]{2,1,0:T(8,128)(2,1)S(1)} %get-tuple-element.52), channel_id=1, source_target_pairs={{4,0},{5,1},{6,2},{7,3},{12,8},{13,9},{14,10},{15,11},{20,16},{21,... | collective-permute-start | bytes 1572872 | tf_op jit(solution)/shard_map/ppermute | solution.py:322

commit v4 on v3

--- a/solution.py
+++ b/solution.py
@@ -119,8 +119,8 @@
     dq_ref, near_ref, far_ref, pair_ref, own_ref = outs
     tok = near_ref.shape[1]
     dv = jnp.dot(probs, u, preferred_element_type=F32)
-    dk = jnp.dot(dscore, q, preferred_element_type=F32) * SCALE
-    dq = lax.dot_general(dscore, keys, TN, preferred_element_type=F32) * SCALE
+    dk = jnp.dot(dscore, q, preferred_element_type=F32)
+    dq = lax.dot_general(dscore, keys, TN, preferred_element_type=F32)
     for g in range(GROUP):
         dq_ref[:, cut(head * GROUP + g, HD)] = dq[cut(g, tok)].astype(BF16)
     cols = cut(head, HD)
@@ -222,6 +222,7 @@
         weight_ref[...] = jnp.broadcast_to(weight, weight_ref.shape)
 
     weight = weight_ref[...]
+    scaled = weight * SCALE
     even = 1.0 - lax.rem(where_ref[1], 2).astype(F32)
     origin = [(part, head) for part, heads in enumerate(HEADS) for head in range(heads)]
     for at in range(len(origin) // PER_STEP):
@@ -231,15 +232,15 @@
             for here in range(PER_STEP):
                 part, local = origin[at * PER_STEP + here]
                 cols, back = cut(local, HD), cut(at * PER_STEP + here, HD)
-                for out, base in ((out_k, 0), (out_v, 1)):
+                for out, base, factor in ((out_k, 0, scaled), (out_v, 1, weight)):
                     side = own_refs[part][base, :, cols]
                     side = side + even * pair_refs[part][1, base, :, cols].astype(F32)
                     side = side + near[base, :, back].astype(F32)
                     side = side + far[base, :, back].astype(F32)
-                    out[:, cut(here, HD)] = (side * weight).astype(BF16)
+                    out[:, cut(here, HD)] = (side * factor).astype(BF16)
                 for g in range(GROUP):
                     dq = dq_refs[part][:, cut(local * GROUP + g, HD)].astype(F32)
-                    out_q[:, cut(here * GROUP + g, HD)] = (dq * weight).astype(BF16)
+                    out_q[:, cut(here * GROUP + g, HD)] = (dq * scaled).astype(BF16)
 
 
 def finish_all(where, small, grad_q, mines, pairs, backs):

time: 82.1 us -> 82 us (level)
  no operation moved by 1% of the time
where the time goes in v4:
time: 82 us; the launch traced here: 81.6 us
  blocking collectives  30.3 us (37%)
  Pallas kernels  24.1 us (29%)
  starting transfers between devices  18.1 us (22%)
  waiting for transfers between devices  4.16 us (5%)
  local copies, waits for them, and re-layouts  3.87 us (5%)
  between operations  0.92 us (1%)
    all_to_all x1, blocking collectives, per_device(): lax.all_to_all(term, ('dp', 'ctx'), split_axis=0, concat_axis=0, tiled=True)  30.3 us
    pallas_call x4, Pallas kernels, local_call(): pl.pallas_call(kernel, in_specs=[SMEM] * scalars + [VMEM] * (len(args) -...  21.1 us
    ppermute x2, starting transfers between devices, per_device(): near.append(lax.ppermute(block, 'ctx', shift(2)))  5.95 us
    ppermute x2, starting transfers between devices, per_device(): far.append(lax.ppermute(block, 'ctx', shift(4)))  5.65 us
    ppermute x6, starting transfers between devices, gather_window(): pairs = [lax.ppermute(array, 'ctx', SIBLING) for array in pairs]  3.13 us
    pallas_call x1, Pallas kernels, finish_all(): pl.pallas_call(finish, grid=(steps,), in_specs=[SMEM] + [VMEM] * len(arra...  2.92 us
    ppermute x6, waiting for transfers between devices, gather_window(): pairs = [lax.ppermute(array, 'ctx', SIBLING) for array in pairs]  2.6 us
    unnamed x26, local copies, waits for them, and re-layouts  2.55 us
  transfers between devices with their start and end apart: 14, of which 6 were waited for; matrix products, arithmetic and copies ran while one was open for 0% of the time, Pallas kernels for 25%

profile of v4, /device:TPU:1, one launch (start us, length us, event | category | flops | bytes accessed | tf_op | source)
XLA Modules:
  0.0 81.6 jit_solution(11785699076266599499)
XLA Ops:
  0.6 1.3 %fusion = (bf16[128,512]{1,0:T(8,128)(2,1)S(1)}, bf16[128,512]{1,0:T(8,128)(2,1)S(1)}, bf16[128,512]{1,0:T(8,128)(2,1)S(1)}, bf16[128,512]{1,0:T(8,128)(2,1)S(1)}) fusion(bf16[128,1024]{1,0:T(8,128)(2,1)} %bitcast.24, bf16[128,1024]{1,0:T(8,128)(2,1)} %bitcast.25), kind=kLoop, calls=%fused_computation.5 | loop fusion | bytes 1048576 | tf_op jit(solution)/shard_map/slice | solution.py:286
  2.0 4.0 %collective-permute-start = (bf16[128,1024]{1,0:T(8,128)(2,1)S(1)}, bf16[128,1024]{1,0:T(8,128)(2,1)S(1)}, u32[]{:S(2)}, u32[]{:S(2)}) collective-permute-start(bf16[128,1024]{1,0:T(8,128)(2,1)S(1)} %pad_maximum_fusion.refs_0_), channel_id=1, source_target_pairs={{0,2},{1,3},{2,4},{3,5},{4,6},{5,7},{8,10},{9,11},{10,12},{11,13},... | collective-permute-start | bytes 786440 | tf_op jit(solution)/shard_map/ppermute | solution.py:288
  6.0 4.4 %collective-permute-start.1 = (bf16[128,1024]{1,0:T(8,128)(2,1)S(1)}, bf16[128,1024]{1,0:T(8,128)(2,1)S(1)}, u32[]{:S(2)}, u32[]{:S(2)}) collective-permute-start(bf16[128,1024]{1,0:T(8,128)(2,1)S(1)} %pad_maximum_fusion.refs_0_), channel_id=1, source_target_pairs={{0,4},{1,5},{2,6},{3,7},{8,12},{9,13},{10,14},{11,15},{16,20},{17,... | collective-permute-start | bytes 786440 | tf_op jit(solution)/shard_map/ppermute | solution.py:289
  10.4 2.0 %collective-permute-start.6 = (bf16[128,1024]{1,0:T(8,128)(2,1)S(1)}, bf16[128,1024]{1,0:T(8,128)(2,1)}, u32[]{:S(2)}, u32[]{:S(2)}) collective-permute-start(bf16[128,1024]{1,0:T(8,128)(2,1)S(1)} %pad_maximum_fusion.1.refs_0_), channel_id=1, source_target_pairs={{0,2},{1,3},{2,4},{3,5},{4,6},{5,7},{8,10},{9,11},{10,12},{11,13},... | collective-permute-start | bytes 786440 | tf_op jit(solution)/shard_map/ppermute | solution.py:288
  12.4 1.3 %collective-permute-start.7 = (bf16[128,1024]{1,0:T(8,128)(2,1)S(1)}, bf16[128,1024]{1,0:T(8,128)(2,1)S(1)}, u32[]{:S(2)}, u32[]{:S(2)}) collective-permute-start(bf16[128,1024]{1,0:T(8,128)(2,1)S(1)} %pad_maximum_fusion.1.refs_0_), channel_id=1, source_target_pairs={{0,4},{1,5},{2,6},{3,7},{8,12},{9,13},{10,14},{11,15},{16,20},{17,... | collective-permute-start | bytes 786440 | tf_op jit(solution)/shard_map/ppermute | solution.py:289
  13.7 0.1 pad_add_fusion.where_ref
  13.8 1.6 %copy-done.1 = bf16[1,128,8192]{2,1,0:T(8,128)(2,1)S(1)} copy-done((bf16[1,128,8192]{2,1,0:T(8,128)(2,1)S(1)}, bf16[1,128,8192]{2,1,0:T(8,128)(2,1)}, u32[]{:S(2)}) %copy-start.1) | copy-done | bytes 2097176
  15.4 0.9 %copy-done.2 = s32[32,1024]{1,0:T(8,128)S(1)} copy-done((s32[32,1024]{1,0:T(8,128)S(1)}, s32[32,1024]{1,0:T(8,128)}, u32[]{:S(2)}) %copy-start.2) | copy-done | bytes 131096
  16.3 1.4 %shard_map.120 = (f32[640,128]{1,0:T(8,128)S(1)}, f32[128,128]{1,0:T(8,128)S(1)}, f32[1,128]{1,0:T(1,128)S(1)}, bf16[4096,128]{1,0:T(8,128)(2,1)S(1)}, bf16[4096...) custom-call(s32[2]{0:T(128)S(1)} %pad_add_fusion.where_ref, ...), custom_call_target="tpu_custom_call" | custom-call | tf_op jit(solution)/shard_map/pallas_call | solution.py:147
  17.8 0.1 broadcast_select_fusion.1
  17.9 1.6 %collective-permute-start.4 = (bf16[64,1024]{1,0:T(8,128)(2,1)S(1)}, bf16[64,1024]{1,0:T(8,128)(2,1)S(1)}, u32[]{:S(2)}, u32[]{:S(2)}) collective-permute-start(bf16[64,1024]{1,0:T(8,128)(2,1)S(1)} %get-tuple-element.69), channel_id=1, source_target_pairs={{0,1},{1,0},{2,3},{3,2},{4,5},{5,4},{6,7},{7,6},{8,9},{9,8},{10,11... | collective-permute-start | bytes 393224 | tf_op jit(solution)/shard_map/ppermute | solution.py:268
  19.4 0.1 collective-permute-start.5
  19.6 0.5 collective-permute-start.2
  20.1 0.4 collective-permute-done.4.refs_5_
  20.4 0.4 collective-permute-start.3
  20.8 0.3 collective-permute-done.2.refs_3_
  21.0 0.7 collective-permute-done.3.refs_4_
  21.8 9.3 %shard_map.121 = (f32[1,128]{1,0:T(1,128)S(1)}, bf16[128,4096]{1,0:T(8,128)(2,1)S(1)}, bf16[2,128,512]{2,1,0:T(8,128)(2,1)S(1)}, bf16[2,128,512]{2,1,0:T(8,128)(...) custom-call(s32[2]{0:T(128)S(1)} %pad_add_fusion.where_ref, s32[32,1024]{1,0:T(8,128)S(1)} %copy-done.2, ...), custom_call_target="tpu_custom_call" | custom-call | flops 1000 | bytes 1000 | tf_op jit(solution)/shard_map/pallas_call | solution.py:147
  31.1 0.1 broadcast_select_fusion
  31.1 0.4 collective-permute-start.9
  31.6 0.1 collective-permute-start.8
  31.7 0.4 collective-permute-start.10
  32.1 0.7 collective-permute-done.9.refs_4_
  32.8 0.6 collective-permute-done.8.refs_3_
  33.3 9.6 %shard_map.122 = (f32[256,128]{1,0:T(8,128)S(1)}, bf16[128,4096]{1,0:T(8,128)(2,1)S(1)}, bf16[2,128,512]{2,1,0:T(8,128)(2,1)S(1)}, bf16[2,128,512]{2,1,0:T(8,128...) custom-call(s32[2]{0:T(128)S(1)} %pad_add_fusion.where_ref, s32[32,1024]{1,0:T(8,128)S(1)} %copy-done.2, ...), custom_call_target="tpu_custom_call" | custom-call | flops 1000 | bytes 1000 | tf_op jit(solution)/shard_map/pallas_call | solution.py:147
  43.0 0.4 collective-permute-start.11
  43.4 1.5 %collective-permute-done.11.refs_5_.refs_11_ = bf16[2,2,128,512]{3,2,1,0:T(8,128)(2,1)S(1)} collective-permute-done((bf16[2,2,128,512]{3,2,1,0:T(8,128)(2,1)S(1)}, bf16[2,2,128,512]{3,2,1,0:T(8,128)(2,1)S(1)}, u32[]{:S(2)}, u32[]{:S(2)}) %collective-permute-start.11) | collective-permute-done | bytes 524320 | tf_op jit(solution)/shard_map/ppermute | solution.py:317
  45.0 0.8 %shard_map.123 = (bf16[2,128,1024]{2,1,0:T(8,128)(2,1)S(1)}, bf16[2,128,1024]{2,1,0:T(8,128)(2,1)S(1)}) custom-call(s32[2]{0:T(128)S(1)} %pad_add_fusion.where_ref, bf16[2,128,512]{2,1,0:T(8,128)(2,1)S(1)} %get-tuple-element.45.refs_0_, bf16[2,128,512]{2,1,0:T(8,128)(2,1)S(1)} %get-tuple-element.46.refs_1_, ...), custom_call_target="tpu_custom_call" | custom-call | flops 1000 | bytes 1000 | tf_op jit(solution)/shard_map/pallas_call | solution.py:147
  45.8 1.3 %collective-permute-start.12 = (bf16[2,128,1024]{2,1,0:T(8,128)(2,1)S(1)}, bf16[2,128,1024]{2,1,0:T(8,128)(2,1)S(1)}, u32[]{:S(2)}, u32[]{:S(2)}) collective-permute-start(bf16[2,128,1024]{2,1,0:T(8,128)(2,1)S(1)} %get-tuple-element.51), channel_id=1, source_target_pairs={{2,0},{3,1},{4,2},{5,3},{6,4},{7,5},{10,8},{11,9},{12,10},{13,11},... | collective-permute-start | bytes 1572872 | tf_op jit(solution)/shard_map/ppermute | solution.py:322
  47.1 1.3 %collective-permute-start.13 = (bf16[2,128,1024]{2,1,0:T(8,128)(2,1)S(1)}, bf16[2,128,1024]{2,1,0:T(8,128)(2,1)S(1)}, u32[]{:S(2)}, u32[]{:S(2)}) collective-permute-start(bf16[2,128,1024]{2,1,0:T(8,128)(2,1)S(1)} %get-tuple-element.52), channel_id=1, source_target_pairs={{4,0},{5,1},{6,2},{7,3},{12,8},{13,9},{14,10},{15,11},{20,16},{21,... | collective-permute-start | bytes 1572872 | tf_op jit(solution)/shard_map/ppermute | solution.py:323
  48.4 30.3 %all_to_all.11 = f32[256,1,128]{2,1,0:T(1,128)S(1)} all-to-all(f32[256,1,128]{2,1,0:T(1,128)S(1)} %bitcast.20), channel_id=1, replica_groups=mesh['dp'=32,'ctx'=8] {'dp','ctx'}, dimensions={0} | all-to-all | bytes 262144 | tf_op jit(solution)/shard_map/all_to_all | solution.py:327
  78.7 2.9 %shard_map.124 = (bf16[128,8192]{1,0:T(8,128)(2,1)}, bf16[128,1024]{1,0:T(8,128)(2,1)}, bf16[128,1024]{1,0:T(8,128)(2,1)}, f32[1,1]{1,0:T(1,128)}) custom-call(s32[2]{0:T(128)S(1)} %pad_add_fusion.where_ref, f32[256,128]{1,0:T(8,128)S(1)} %bitcast.19, f32[1,128]{1,0:T(1,128)S(1)} %get-tuple-element.54.refs_1_, f32[128,128]{1,0:T(8,128)S(1)} %get-tuple-element.55.refs_2_, ...), custom_call_target="tpu_custom_call" | custom-call | tf_op jit(solution)/shard_map/pallas_call | solution.py:251
  (36 shorter events, 0.2 us)
Async XLA Ops:
  0.6 13.1 %copy-start = (bf16[1,128,8192]{2,1,0:T(8,128)(2,1)S(1)}, bf16[1,128,8192]{2,1,0:T(8,128)(2,1)}, u32[]{:S(2)}) copy-start(bf16[1,128,8192]{2,1,0:T(8,128)(2,1)} %param.9) | copy-start | bytes 6291460
  1.9 8.4 %copy-start.9 = (bf16[128,512]{1,0:T(8,128)(2,1)}, bf16[128,512]{1,0:T(8,128)(2,1)S(1)}, u32[]{:S(2)}) copy-start(bf16[128,512]{1,0:T(8,128)(2,1)S(1)} %get-tuple-element.65) | copy-start | bytes 393220
  1.9 8.4 %copy-start.11 = (bf16[128,512]{1,0:T(8,128)(2,1)}, bf16[128,512]{1,0:T(8,128)(2,1)S(1)}, u32[]{:S(2)}) copy-start(bf16[128,512]{1,0:T(8,128)(2,1)S(1)} %get-tuple-element.72) | copy-start | bytes 393220
  1.9 8.4 %copy-start.7 = (bf16[128,512]{1,0:T(8,128)(2,1)}, bf16[128,512]{1,0:T(8,128)(2,1)S(1)}, u32[]{:S(2)}) copy-start(bf16[128,512]{1,0:T(8,128)(2,1)S(1)} %get-tuple-element.73) | copy-start | bytes 393220
  2.0 15.7 %collective-permute-start = (bf16[128,1024]{1,0:T(8,128)(2,1)S(1)}, bf16[128,1024]{1,0:T(8,128)(2,1)S(1)}, u32[]{:S(2)}, u32[]{:S(2)}) collective-permute-start(bf16[128,1024]{1,0:T(8,128)(2,1)S(1)} %pad_maximum_fusion.refs_0_), channel_id=1, source_target_pairs={{0,2},{1,3},{2,4},{3,5},{4,6},{5,7},{8,10},{9,11},{10,12},{11,13},... | collective-permute-start | bytes 786440 | tf_op jit(solution)/shard_map/ppermute | solution.py:288
  6.0 11.8 %collective-permute-start.1 = (bf16[128,1024]{1,0:T(8,128)(2,1)S(1)}, bf16[128,1024]{1,0:T(8,128)(2,1)S(1)}, u32[]{:S(2)}, u32[]{:S(2)}) collective-permute-start(bf16[128,1024]{1,0:T(8,128)(2,1)S(1)} %pad_maximum_fusion.refs_0_), channel_id=1, source_target_pairs={{0,4},{1,5},{2,6},{3,7},{8,12},{9,13},{10,14},{11,15},{16,20},{17,... | collective-permute-start | bytes 786440 | tf_op jit(solution)/shard_map/ppermute | solution.py:289
  10.4 20.7 %collective-permute-start.6 = (bf16[128,1024]{1,0:T(8,128)(2,1)S(1)}, bf16[128,1024]{1,0:T(8,128)(2,1)}, u32[]{:S(2)}, u32[]{:S(2)}) collective-permute-start(bf16[128,1024]{1,0:T(8,128)(2,1)S(1)} %pad_maximum_fusion.1.refs_0_), channel_id=1, source_target_pairs={{0,2},{1,3},{2,4},{3,5},{4,6},{5,7},{8,10},{9,11},{10,12},{11,13},... | collective-permute-start | bytes 786440 | tf_op jit(solution)/shard_map/ppermute | solution.py:288
  12.4 18.7 %collective-permute-start.7 = (bf16[128,1024]{1,0:T(8,128)(2,1)S(1)}, bf16[128,1024]{1,0:T(8,128)(2,1)S(1)}, u32[]{:S(2)}, u32[]{:S(2)}) collective-permute-start(bf16[128,1024]{1,0:T(8,128)(2,1)S(1)} %pad_maximum_fusion.1.refs_0_), channel_id=1, source_target_pairs={{0,4},{1,5},{2,6},{3,7},{8,12},{9,13},{10,14},{11,15},{16,20},{17,... | collective-permute-start | bytes 786440 | tf_op jit(solution)/shard_map/ppermute | solution.py:289
  13.8 1.6 %copy-start.1 = (bf16[1,128,8192]{2,1,0:T(8,128)(2,1)S(1)}, bf16[1,128,8192]{2,1,0:T(8,128)(2,1)}, u32[]{:S(2)}) copy-start(bf16[1,128,8192]{2,1,0:T(8,128)(2,1)} %param.12) | copy-start | bytes 6291460
  15.4 0.9 %copy-start.2 = (s32[32,1024]{1,0:T(8,128)S(1)}, s32[32,1024]{1,0:T(8,128)}, u32[]{:S(2)}) copy-start(s32[32,1024]{1,0:T(8,128)} %seg_ref.5) | copy-start | bytes 393220
  16.3 1.5 %copy-start.10 = (bf16[128,512]{1,0:T(8,128)(2,1)S(1)}, bf16[128,512]{1,0:T(8,128)(2,1)}, u32[]{:S(2)}) copy-start(bf16[128,512]{1,0:T(8,128)(2,1)} %copy-done.9) | copy-start | bytes 393220
  16.3 1.5 %copy-start.12 = (bf16[128,512]{1,0:T(8,128)(2,1)S(1)}, bf16[128,512]{1,0:T(8,128)(2,1)}, u32[]{:S(2)}) copy-start(bf16[128,512]{1,0:T(8,128)(2,1)} %copy-done.11) | copy-start | bytes 393220
  16.3 5.5 %copy-start.3 = (f32[1,128]{1,0:T(1,128)S(1)}, f32[1,128]{1,0:T(1,128)}, u32[]{:S(2)}) copy-start(f32[1,128]{1,0:T(1,128)} %term_in.1) | copy-start | bytes 1540
  17.9 2.6 %collective-permute-start.4 = (bf16[64,1024]{1,0:T(8,128)(2,1)S(1)}, bf16[64,1024]{1,0:T(8,128)(2,1)S(1)}, u32[]{:S(2)}, u32[]{:S(2)}) collective-permute-start(bf16[64,1024]{1,0:T(8,128)(2,1)S(1)} %get-tuple-element.69), channel_id=1, source_target_pairs={{0,1},{1,0},{2,3},{3,2},{4,5},{5,4},{6,7},{7,6},{8,9},{9,8},{10,11... | collective-permute-start | bytes 393224 | tf_op jit(solution)/shard_map/ppermute | solution.py:268
  19.4 11.6 %copy-start.8 = (bf16[128,512]{1,0:T(8,128)(2,1)S(1)}, bf16[128,512]{1,0:T(8,128)(2,1)}, u32[]{:S(2)}) copy-start(bf16[128,512]{1,0:T(8,128)(2,1)} %copy-done.7) | copy-start | bytes 393220
  19.4 1.4 %collective-permute-start.5 = (bf16[64,1024]{1,0:T(8,128)(2,1)S(1)}, bf16[64,1024]{1,0:T(8,128)(2,1)S(1)}, u32[]{:S(2)}, u32[]{:S(2)}) collective-permute-start(bf16[64,1024]{1,0:T(8,128)(2,1)S(1)} %get-tuple-element.68), channel_id=1, source_target_pairs={{0,1},{1,0},{2,3},{3,2},{4,5},{5,4},{6,7},{7,6},{8,9},{9,8},{10,11... | collective-permute-start | bytes 393224 | tf_op jit(solution)/shard_map/ppermute | solution.py:268
  19.6 1.5 %collective-permute-start.2 = (bf16[64,1024]{1,0:T(8,128)(2,1)S(1)}, bf16[64,1024]{1,0:T(8,128)(2,1)S(1)}, u32[]{:S(2)}, u32[]{:S(2)}) collective-permute-start(bf16[64,1024]{1,0:T(8,128)(2,1)S(1)} %get-tuple-element.71), channel_id=1, source_target_pairs={{0,1},{1,0},{2,3},{3,2},{4,5},{5,4},{6,7},{7,6},{8,9},{9,8},{10,11... | collective-permute-start | bytes 393224 | tf_op jit(solution)/shard_map/ppermute | solution.py:268
  20.4 1.3 %collective-permute-start.3 = (bf16[64,1024]{1,0:T(8,128)(2,1)S(1)}, bf16[64,1024]{1,0:T(8,128)(2,1)S(1)}, u32[]{:S(2)}, u32[]{:S(2)}) collective-permute-start(bf16[64,1024]{1,0:T(8,128)(2,1)S(1)} %get-tuple-element.70), channel_id=1, source_target_pairs={{0,1},{1,0},{2,3},{3,2},{4,5},{5,4},{6,7},{7,6},{8,9},{9,8},{10,11... | collective-permute-start | bytes 393224 | tf_op jit(solution)/shard_map/ppermute | solution.py:268
  31.1 1.6 %collective-permute-start.9 = (bf16[128,1024]{1,0:T(8,128)(2,1)S(1)}, bf16[128,1024]{1,0:T(8,128)(2,1)S(1)}, u32[]{:S(2)}, u32[]{:S(2)}) collective-permute-start(bf16[128,1024]{1,0:T(8,128)(2,1)S(1)} %broadcast_select_fusion), channel_id=1, source_target_pairs={{0,1},{1,0},{2,3},{3,2},{4,5},{5,4},{6,7},{7,6},{8,9},{9,8},{10,11... | collective-permute-start | bytes 786440 | tf_op jit(solution)/shard_map/ppermute | solution.py:268
  31.6 1.8 %collective-permute-start.8 = (bf16[128,1024]{1,0:T(8,128)(2,1)}, bf16[128,1024]{1,0:T(8,128)(2,1)S(1)}, u32[]{:S(2)}, u32[]{:S(2)}) collective-permute-start(bf16[128,1024]{1,0:T(8,128)(2,1)} %collective-permute-done.6.refs_1_), channel_id=1, source_target_pairs={{0,1},{1,0},{2,3},{3,2},{4,5},{5,4},{6,7},{7,6},{8,9},{9,8},{10,11... | collective-permute-start | bytes 786440 | tf_op jit(solution)/shard_map/ppermute | solution.py:268
  31.7 11.7 %collective-permute-start.10 = (bf16[2,2,128,512]{3,2,1,0:T(8,128)(2,1)S(1)}, bf16[2,2,128,512]{3,2,1,0:T(8,128)(2,1)S(1)}, u32[]{:S(2)}, u32[]{:S(2)}) collective-permute-start(bf16[2,2,128,512]{3,2,1,0:T(8,128)(2,1)S(1)} %get-tuple-element.47), channel_id=1, source_target_pairs={{0,1},{1,0},{2,3},{3,2},{4,5},{5,4},{6,7},{7,6},{8,9},{9,8},{10,11... | collective-permute-start | bytes 1572872 | tf_op jit(solution)/shard_map/ppermute | solution.py:317
  42.9 35.7 %copy-start.4 = (s32[128]{0:T(128)S(1)}, s32[128]{0:T(128)}, u32[]{:S(2)}) copy-start(s32[128]{0:T(128)} %param.15) | copy-start | bytes 1540
  43.0 35.7 %copy-start.5 = (s32[128]{0:T(128)S(1)}, s32[128]{0:T(128)}, u32[]{:S(2)}) copy-start(s32[128]{0:T(128)} %param.16) | copy-start | bytes 1540
  43.0 35.7 %copy-start.6 = (f32[128]{0:T(128)S(1)}, f32[128]{0:T(128)}, u32[]{:S(2)}) copy-start(f32[128]{0:T(128)} %param.17) | copy-start | bytes 1540
  43.0 2.0 %collective-permute-start.11 = (bf16[2,2,128,512]{3,2,1,0:T(8,128)(2,1)S(1)}, bf16[2,2,128,512]{3,2,1,0:T(8,128)(2,1)S(1)}, u32[]{:S(2)}, u32[]{:S(2)}) collective-permute-start(bf16[2,2,128,512]{3,2,1,0:T(8,128)(2,1)S(1)} %get-tuple-element.50), channel_id=1, source_target_pairs={{0,1},{1,0},{2,3},{3,2},{4,5},{5,4},{6,7},{7,6},{8,9},{9,8},{10,11... | collective-permute-start | bytes 1572872 | tf_op jit(solution)/shard_map/ppermute | solution.py:317
  45.8 32.9 %collective-permute-start.12 = (bf16[2,128,1024]{2,1,0:T(8,128)(2,1)S(1)}, bf16[2,128,1024]{2,1,0:T(8,128)(2,1)S(1)}, u32[]{:S(2)}, u32[]{:S(2)}) collective-permute-start(bf16[2,128,1024]{2,1,0:T(8,128)(2,1)S(1)} %get-tuple-element.51), channel_id=1, source_target_pairs={{2,0},{3,1},{4,2},{5,3},{6,4},{7,5},{10,8},{11,9},{12,10},{13,11},... | collective-permute-start | bytes 1572872 | tf_op jit(solution)/shard_map/ppermute | solution.py:322
  47.1 31.6 %collective-permute-start.13 = (bf16[2,128,1024]{2,1,0:T(8,128)(2,1)S(1)}, bf16[2,128,1024]{2,1,0:T(8,128)(2,1)S(1)}, u32[]{:S(2)}, u32[]{:S(2)}) collective-permute-start(bf16[2,128,1024]{2,1,0:T(8,128)(2,1)S(1)} %get-tuple-element.52), channel_id=1, source_target_pairs={{4,0},{5,1},{6,2},{7,3},{12,8},{13,9},{14,10},{15,11},{20,16},{21,... | collective-permute-start | bytes 1572872 | tf_op jit(solution)/shard_map/ppermute | solution.py:323
